TPU v7x, 32 devices: a whole 2x2x4 slice. The times are simulated.
32 devices in a mesh: gx: 8 (over z, y), gy: 4 (over x, core).
Axes of the slice: x: 2, y: 2, z: 4, core: 2. Of those that a mesh axis runs over, the one named last changes fastest.
Arguments:
- temper_start: float32 [256, 256, 256], P('gx', 'gy'), may hold values from -4 to 4
- cure_start: float32 [256, 256, 256], P('gx', 'gy'), may hold values from 0.05 to 0.9
- temper_middle: float32 [256, 256, 256], P('gx', 'gy'), may hold values from -4 to 4
- cure_middle: float32 [256, 256, 256], P('gx', 'gy'), may hold values from 0.05 to 0.9
- adjoint_temper: float32 [256, 256, 256], P('gx', 'gy'), may hold values from -6 to 6
- adjoint_cure: float32 [256, 256, 256], P('gx', 'gy'), may hold values from -6 to 6
- conduct_first: float32 [264], P('gx'), may hold values from 0 to 3000, as said below
- inverse_first: float32 [256, 32], P('gx'), may hold values from 0 to 1, as said below
- conduct_second: float32 [260], P('gy'), may hold values from 0 to 3000, as said below
- inverse_second: float32 [256, 64], P('gy'), may hold values from 0 to 1, as said below
- conduct_thick: float32 [257], replicated, may hold values from 20 to 120
- inverse_thick: float32 [256, 256], replicated, may hold values from 0 to 1, as said below
Outputs:
- sensitivity_temper: float32 [256, 256, 256], P('gx', 'gy')
- sensitivity_cure: float32 [256, 256, 256], P('gx', 'gy')
Inputs may be any that keep to these rules, and one draw needn't show every extreme that they name: `conduct_first`: group j of 33 entries holds the left faces of its 32 cells and then the face beyond them; entry 32 of group j equals entry 0 of group j + 1, and the last group's entry 32 is 0 (insulated side). `inverse_first`: rows j * 32 to (j + 1) * 32 - 1 are the inverse of group j's diagonal block of I + Kx restricted to that group: diagonal 1 plus the cell's two faces, off-diagonals minus the faces between its cells. `conduct_second`: group j of 65 entries holds the left faces of its 64 cells and then the face beyond them; entry 64 of group j equals entry 0 of group j + 1, and the last group's entry 64 is 0 (insulated side). `inverse_second`: rows j * 64 to (j + 1) * 64 - 1 are the inverse of group j's diagonal block of I + Ky restricted to that group. `inverse_thick`: the inverse of I + Kz through the thickness.
All inputs are finite; a program needn't handle non-finite values.
Results may differ from a plain program's by a relative error of at most 0.0003.
Values sent between devices are 32-bit elements; how exact they have to be, the bound alone decides.
A program may use at most 128 MiB of HBM per device.

v0:
```python
import jax
import jax.numpy as jnp
from jax import lax
from jax.sharding import PartitionSpec as P

explicit_part = 2.0
heat_release = 100.0
cure_step = 0.5
arrhenius = 0.5
initial_rate = 0.1
highest = lax.Precision.HIGHEST


def extended(block, sides, width):
    for axis, dim in sides:
        count = lax.axis_size(axis)
        forward = [(i, i + 1) for i in range(count - 1)]
        backward = [(target, source) for source, target in forward]
        low = lax.ppermute(
            lax.slice_in_dim(block, block.shape[dim] - width, None, axis=dim), axis, forward
        )
        high = lax.ppermute(lax.slice_in_dim(block, 0, width, axis=dim), axis, backward)
        block = jnp.concatenate([low, block, high], axis=dim)
    return block


def reduced_solve(first_tip, last_tip, spike_ends):
    empty_row = jnp.zeros_like(first_tip[:1])

    def forward(running, inputs):
        corner_prev, partial_prev = running
        tail_here, head_next, left_here, right_here, value_last, value_first = inputs
        upper_entry = -tail_here - left_here * right_here * corner_prev
        lower_entry = -head_next
        determinant = 1.0 - upper_entry * lower_entry
        corner = -upper_entry / determinant
        bottom = 1.0 / determinant
        shifted = value_last + left_here * partial_prev
        solved_top = bottom * shifted + corner * value_first
        solved_low = -lower_entry / determinant * shifted + bottom * value_first
        return ((corner, solved_top), (solved_top, solved_low, corner, bottom))

    start_state = (jnp.zeros((), jnp.float32), jnp.zeros_like(first_tip[0]))
    inputs = (
        spike_ends[:-1, 3],
        spike_ends[1:, 0],
        spike_ends[:-1, 1],
        spike_ends[:-1, 2],
        last_tip[:-1],
        first_tip[1:],
    )
    unused, (tops, lows, corners, bottoms) = lax.scan(forward, start_state, inputs)

    def backward(next_low, inputs):
        solved_top, solved_low, corner, bottom, right_next = inputs
        top_value = solved_top + corner * right_next * next_low
        low_value = solved_low + bottom * right_next * next_low
        return (low_value, (top_value, low_value))

    unused, (top_values, low_values) = lax.scan(
        backward,
        jnp.zeros_like(first_tip[0]),
        (tops, lows, corners, bottoms, spike_ends[1:, 2]),
        reverse=True,
    )
    next_first = jnp.concatenate([low_values, empty_row], axis=0)
    prev_last = jnp.concatenate([empty_row, top_values], axis=0)
    return (next_first, prev_last)


def reduced_maps(spike_ends):
    count = spike_ends.shape[0]
    identity = jnp.eye(2 * count, dtype=jnp.float32)
    next_map, prev_map = reduced_solve(identity[0::2], identity[1::2], spike_ends)
    both_map = jnp.stack([next_map, prev_map], axis=1).reshape(2 * count, 2 * count)
    return (next_map, prev_map, both_map)


def spike_summary(left_spike, right_spike):
    return jnp.stack([left_spike[0], left_spike[-1], right_spike[0], right_spike[-1]])


def first_reduced(tip_rows, maps):
    next_map, prev_map, both_map = maps
    groups = lax.axis_size("gx")
    lines = tip_rows.shape[1]
    pieces = tip_rows.reshape(2, groups, lines // groups)[None]
    tips = lax.all_to_all(pieces, "gx", split_axis=2, concat_axis=0, tiled=True).reshape(
        2 * groups, -1
    )
    solved = jnp.dot(both_map, tips, precision=highest)
    answer = solved.reshape(groups, 2, 1, -1)
    returned = lax.all_to_all(answer, "gx", split_axis=0, concat_axis=2, tiled=True)
    solved = returned.reshape(2, lines)
    return (solved[0], solved[1])


def second_reduced(tip_rows, maps):
    next_map, prev_map, both_map = maps
    groups = lax.axis_size("gy")
    lines = tip_rows.shape[1]
    pieces = tip_rows.reshape(2, groups, lines // groups)[None]
    tips = lax.all_to_all(pieces, "gy", split_axis=2, concat_axis=0, tiled=True).reshape(
        2 * groups, -1
    )
    solved = jnp.dot(both_map, tips, precision=highest)
    answer = solved.reshape(groups, 2, 1, -1)
    returned = lax.all_to_all(answer, "gy", split_axis=0, concat_axis=2, tiled=True)
    solved = returned.reshape(2, lines)
    return (solved[0], solved[1])


def solve_first(right_side, inverse, left_spike, right_spike, maps):
    rows_first, rows_second, depth = right_side.shape
    blockwise = jnp.einsum(
        "ba,bl->al", inverse, right_side.reshape(rows_first, -1), precision=highest
    )
    tip_rows = jnp.stack([blockwise[0], blockwise[-1]])
    next_first, prev_last = first_reduced(tip_rows, maps)
    result = (
        blockwise
        + left_spike[:, None] * prev_last[None, :]
        + right_spike[:, None] * next_first[None, :]
    )
    return (
        result.reshape(rows_first, rows_second, depth),
        next_first.reshape(rows_second, depth),
        prev_last.reshape(rows_second, depth),
    )


def solve_second(right_side, inverse, left_spike, right_spike, maps):
    rows_first, rows_second, depth = right_side.shape
    blockwise = jnp.einsum("ba,ibl->ial", inverse, right_side, precision=highest)
    tip_rows = jnp.stack([blockwise[:, 0], blockwise[:, -1]]).reshape(2, -1)
    next_first, prev_last = second_reduced(tip_rows, maps)
    next_first = next_first.reshape(rows_first, 1, depth)
    prev_last = prev_last.reshape(rows_first, 1, depth)
    return (
        blockwise + left_spike[None, :, None] * prev_last + right_spike[None, :, None] * next_first
    )


def stiffness(
    field,
    below_first,
    above_first,
    below_second,
    above_second,
    conduct_first,
    conduct_second,
    conduct_thick,
):
    lower = jnp.concatenate([below_first[None], field[:-1]], axis=0)
    upper = jnp.concatenate([field[1:], above_first[None]], axis=0)
    total = conduct_first[:-1][:, None, None] * (field - lower) + conduct_first[1:][
        :, None, None
    ] * (field - upper)
    lower = jnp.concatenate([below_second[:, None], field[:, :-1]], axis=1)
    upper = jnp.concatenate([field[:, 1:], above_second[:, None]], axis=1)
    total = total + (
        conduct_second[:-1][None, :, None] * (field - lower)
        + conduct_second[1:][None, :, None] * (field - upper)
    )
    zero_layer = jnp.zeros_like(field[:, :, :1])
    lower = jnp.concatenate([zero_layer, field[:, :, :-1]], axis=2)
    upper = jnp.concatenate([field[:, :, 1:], zero_layer], axis=2)
    return total + (
        conduct_thick[:-1][None, None, :] * (field - lower)
        + conduct_thick[1:][None, None, :] * (field - upper)
    )


def per_device(
    temper_start,
    cure_start,
    temper_middle,
    cure_middle,
    adjoint_temper,
    adjoint_cure,
    conduct_first,
    inverse_first,
    conduct_second,
    inverse_second,
    conduct_thick,
    inverse_thick,
):
    left_first = conduct_first[0] * inverse_first[0, :]
    right_first = conduct_first[-1] * inverse_first[-1, :]
    ends_first = lax.all_gather(
        spike_summary(left_first, right_first)[None], "gx", axis=0, tiled=True
    )
    left_second = conduct_second[0] * inverse_second[0, :]
    right_second = conduct_second[-1] * inverse_second[-1, :]
    ends_second = lax.all_gather(
        spike_summary(left_second, right_second)[None], "gy", axis=0, tiled=True
    )
    maps_first = reduced_maps(ends_first)
    maps_second = reduced_maps(ends_second)
    temp_adjoint = adjoint_temper
    cure_adjoint = adjoint_cure
    for temper, cure in ((temper_middle, cure_middle), (temper_start, cure_start)):
        heating = jnp.exp(arrhenius * temper)
        remain = 1.0 - cure
        rate = heating * (initial_rate + cure) * remain * remain
        rate_temp = arrhenius * rate
        rate_cure = heating * (remain * remain - 2.0 * (initial_rate + cure) * remain)
        rows_first, rows_second, depth = temp_adjoint.shape
        through = jnp.dot(
            temp_adjoint.reshape(-1, depth), inverse_thick, precision=highest
        ).reshape(rows_first, rows_second, depth)
        second_done = solve_second(through, inverse_second, left_second, right_second, maps_second)
        adjoint_flux, next_first, prev_last = solve_first(
            second_done, inverse_first, left_first, right_first, maps_first
        )
        padded = extended(adjoint_flux, (("gx", 0), ("gy", 1)), 1)
        kick = stiffness(
            adjoint_flux,
            padded[0, 1:-1],
            padded[-1, 1:-1],
            padded[1:-1, 0],
            padded[1:-1, -1],
            conduct_first,
            conduct_second,
            conduct_thick,
        )
        source = heat_release * adjoint_flux + cure_step * cure_adjoint
        temp_adjoint = temp_adjoint - explicit_part * kick + rate_temp * source
        cure_adjoint = cure_adjoint + rate_cure * source
    return (temp_adjoint, cure_adjoint)


def solution(mesh):
    placed = (
        P("gx", "gy", None),
        P("gx", "gy", None),
        P("gx", "gy", None),
        P("gx", "gy", None),
        P("gx", "gy", None),
        P("gx", "gy", None),
        P("gx"),
        P("gx", None),
        P("gy"),
        P("gy", None),
        P(),
        P(),
    )
    return jax.shard_map(
        per_device,
        mesh=mesh,
        in_specs=placed,
        out_specs=(P("gx", "gy", None), P("gx", "gy", None)),
        check_vma=False,
    )
```

profile of v0, /device:TPU:0, one launch (start us, length us, event | category | flops | bytes accessed | tf_op | source)
XLA Modules:
  0.0 311.6 jit_solution(4154412811778701876)
XLA Ops:
  0.7 0.9 copy-done
  1.6 3.5 %fusion.36 = f32[32,64,256]{2,1,0:T(8,128)S(1)} fusion(f32[32,64,256]{2,1,0:T(8,128)} %param.24, f32[256,256]{1,0:T(8,128)S(1)} %copy-done), kind=kOutput, calls=%fused_computation.78 | convolution fusion | flops 1610612736 | bytes 4456448 | tf_op jit(solution)/shard_map/dot_general | solution.py:209
  5.2 2.0 convolution_bitcast_fusion.7
  7.2 0.7 pad_maximum_fusion.2
  7.9 4.2 %all-to-all-start = ((f32[1,2,4,2048]{3,1,0,2:T(2,128)}), f32[1,2,4,2048]{3,1,0,2:T(2,128)S(1)}, u32[]{:S(2)}, u32[]{:S(2)}) async-start(f32[1,2,4,2048]{3,1,0,2:T(2,128)} %pad_maximum_fusion.2), calls=%async_computation | async-start | bytes 131072 | tf_op jit(solution)/shard_map/all_to_all | solution.py:103
  12.9 1.3 slice_multiply_fusion.3
  16.0 2.8 maximum_dynamic-update-slice_fusion
  18.8 7.4 %all-reduce.8 = f32[16]{0:T(128)S(1)} all-reduce(f32[16]{0:T(128)S(1)} %maximum_dynamic-update-slice_fusion), channel_id=2, replica_groups=mesh['gx'=8,'gy'=4] {'gy'}, use_global_device_ids=true, to_apply=%add.8 | all-reduce | flops 16 | bytes 128
  26.6 20.1 %while.80 = (s32[]{:T(128)}, f32[]{:T(128)}, f32[8]{0:T(128)S(1)}, f32[3,8]{1,0:T(4,128)S(1)}, f32[3,8]{1,0:T(4,128)S(1)}, /*index=5*/f32[3]{0:T(128)S(1)}, f32[...) while((s32[]{:T(128)}, f32[]{:T(128)}, f32[8]{0:T(128)S(1)}, ...), condition=%wide.region_1.2_spmd.clone, body=%wide.region_0.1_spmd.clone.sunk | while | flops 86 | bytes 3211 | solution.py:52
  32.3 0.7 fusion.85
  39.0 0.7 fusion.85
  45.7 0.7 fusion.85
  46.7 13.8 %while.81 = (s32[]{:T(128)}, f32[8]{0:T(128)S(1)}, f32[3,8]{1,0:T(4,128)S(1)}, f32[3,8]{1,0:T(4,128)S(1)}, f32[3,8]{1,0:T(4,128)S(1)}, /*index=5*/f32[3]{0:T(128...) while((s32[]{:T(128)}, f32[8]{0:T(128)S(1)}, ...), condition=%wide.region_3.4_spmd.clone, body=%wide.region_2.3_spmd.clone.sunk | while | flops 46 | bytes 507 | solution.py:60
  49.2 0.7 dynamic_slice.205
  62.3 1.2 slice_multiply_fusion.1
  64.2 2.7 maximum_dynamic-update-slice_fusion.1
  66.9 22.2 %all-reduce.9 = f32[32]{0:T(128)S(1)} all-reduce(f32[32]{0:T(128)S(1)} %maximum_dynamic-update-slice_fusion.1), channel_id=3, replica_groups=mesh['gx'=8,'gy'=4] {'gx'}, use_global_device_ids=true, to_apply=%add.9 | all-reduce | flops 32 | bytes 256
  89.4 46.7 %while.82 = (s32[]{:T(128)}, f32[]{:T(128)}, f32[16]{0:T(128)S(1)}, f32[7,16]{1,0:T(8,128)S(1)}, f32[7,16]{1,0:T(8,128)S(1)}, /*index=5*/f32[7]{0:T(128)S(1)}, f...) while((s32[]{:T(128)}, f32[]{:T(128)}, f32[16]{0:T(128)S(1)}, ...), condition=%wide.region_5.6_spmd.clone, body=%wide.region_4.5_spmd.clone.sunk | while | flops 158 | bytes 3499 | solution.py:52
  136.1 31.2 %while.83 = (s32[]{:T(128)}, f32[16]{0:T(128)S(1)}, f32[7,16]{1,0:T(8,128)S(1)}, f32[7,16]{1,0:T(8,128)S(1)}, f32[7,16]{1,0:T(8,128)S(1)}, /*index=5*/f32[7]{0:T...) while((s32[]{:T(128)}, f32[16]{0:T(128)S(1)}, ...), condition=%wide.region_7.8_spmd.clone, body=%wide.region_6.7_spmd.clone.sunk | while | flops 86 | bytes 795 | solution.py:60
  167.6 0.7 copy.29
  168.3 3.3 %all-to-all-start.1 = ((f32[4,2,1,2048]{3,1,2,0:T(2,128)}), f32[4,2,1,2048]{3,1,2,0:T(2,128)S(1)}, u32[]{:S(2)}, u32[]{:S(2)}) async-start(f32[4,2,1,2048]{3,1,2,0:T(2,128)} %copy.29), calls=%async_computation.1 | async-start | bytes 131072 | tf_op jit(solution)/shard_map/all_to_all | solution.py:108
  171.6 4.1 %all-to-all-done.1 = f32[4,2,1,2048]{3,1,2,0:T(2,128)S(1)} async-done(((f32[4,2,1,2048]{3,1,2,0:T(2,128)}), f32[4,2,1,2048]{3,1,2,0:T(2,128)S(1)}, u32[]{:S(2)}, u32[]{:S(2)}) %all-to-all-start.1) | async-done | bytes 65568 | tf_op jit(solution)/shard_map/all_to_all | solution.py:108
  176.3 1.2 copy.42
  177.5 1.9 convolution_bitcast_fusion.1
  179.6 0.8 pad_maximum_fusion
  180.3 3.4 %all-to-all-start.2 = ((f32[1,2,8,2048]{3,1,0,2:T(2,128)}), f32[1,2,8,2048]{3,1,0,2:T(2,128)S(1)}, u32[]{:S(2)}, u32[]{:S(2)}) async-start(f32[1,2,8,2048]{3,1,0,2:T(2,128)} %bitcast.33), calls=%async_computation.2 | async-start | bytes 262144 | tf_op jit(solution)/shard_map/all_to_all | solution.py:88
  183.8 7.2 %all-to-all-done.2 = f32[1,2,8,2048]{3,1,0,2:T(2,128)S(1)} async-done(((f32[1,2,8,2048]{3,1,0,2:T(2,128)}), f32[1,2,8,2048]{3,1,0,2:T(2,128)S(1)}, u32[]{:S(2)}, u32[]{:S(2)}) %all-to-all-start.2) | async-done | bytes 131104 | tf_op jit(solution)/shard_map/all_to_all | solution.py:88
  191.3 0.8 copy.31
  192.1 3.6 %all-to-all-start.3 = ((f32[8,2,1,2048]{3,1,2,0:T(2,128)}), f32[8,2,1,2048]{3,1,2,0:T(2,128)S(1)}, u32[]{:S(2)}, u32[]{:S(2)}) async-start(f32[8,2,1,2048]{3,1,2,0:T(2,128)} %copy.31), calls=%async_computation.3 | async-start | bytes 262144 | tf_op jit(solution)/shard_map/all_to_all | solution.py:93
  195.8 7.0 %all-to-all-done.3 = f32[8,2,1,2048]{3,1,2,0:T(2,128)S(1)} async-done(((f32[8,2,1,2048]{3,1,2,0:T(2,128)}), f32[8,2,1,2048]{3,1,2,0:T(2,128)S(1)}, u32[]{:S(2)}, u32[]{:S(2)}) %all-to-all-start.3) | async-done | bytes 131104 | tf_op jit(solution)/shard_map/all_to_all | solution.py:93
  203.6 2.4 fusion.55
  206.0 2.1 collective-permute-start
  208.1 2.2 copy.43
  210.4 1.3 collective-permute-start.1
  211.7 0.7 fusion.53
  212.6 4.0 %collective-permute-done.1 = f32[1,64,256]{2,1,0:T(8,128)S(1)} collective-permute-done((f32[1,64,256]{2,1,0:T(8,128)S(1)}, f32[1,64,256]{2,1,0:T(8,128)S(1)}, u32[]{:S(2)}, u32[]{:S(2)}) %collective-permute-start.1) | collective-permute-done | bytes 65568 | tf_op jit(solution)/shard_map/ppermute | solution.py:22
  216.6 1.3 collective-permute-start.2
  217.9 1.4 collective-permute-start.3
  220.7 1.4 copy-done.11
  224.3 0.8 copy-done.13
  225.7 3.7 %fusion.10 = f32[32,64,256]{2,1,0:T(8,128)S(1)} fusion(f32[32,64,256]{2,1,0:T(8,128)S(1)} %copy-done.18, f32[31,64,256]{2,1,0:T(8,128)S(1)} %slice.438, f32[1,64,256]{2,1,0:T(8,128)S(1)} %collective-permute-done, f32[1,64,256]{2,1,0:T(8,128)S(1)} %collective-permute-done.1, f32[31,64,256]{2,1,0:T(8,128)S(1)} %slice.439, ...), kind=kLoop, calls=%fused_computation.32 | loop fusion | flops 18350080 | bytes 25152256 | tf_op jit(solution)/shard_map/add | solution.py:228
  229.5 1.9 fusion.34
  231.4 2.0 convolution_bitcast_fusion.6
  233.4 1.3 copy-done.8
  234.8 8.3 %all_to_all.120 = f32[1,2,4,2048]{3,1,0,2:T(2,128)S(1)} all-to-all(f32[1,2,4,2048]{3,1,0,2:T(2,128)S(1)} %pad_maximum_fusion.3), channel_id=1, replica_groups=mesh['gx'=8,'gy'=4] {'gy'}, dimensions={2} | all-to-all | bytes 131072 | tf_op jit(solution)/shard_map/all_to_all | solution.py:103
  243.5 6.5 %all_to_all.121 = f32[4,2,1,2048]{3,1,2,0:T(2,128)S(1)} all-to-all(f32[4,2,1,2048]{3,1,2,0:T(2,128)S(1)} %copy.35), channel_id=1, replica_groups=mesh['gx'=8,'gy'=4] {'gy'}, dimensions={0} | all-to-all | bytes 131072 | tf_op jit(solution)/shard_map/all_to_all | solution.py:108
  250.2 2.0 multiply_add_fusion.4
  252.2 1.2 copy.46
  253.4 1.9 convolution_bitcast_fusion
  255.4 1.3 copy-done.7
  256.9 11.1 %all_to_all.122 = f32[1,2,8,2048]{3,1,0,2:T(2,128)S(1)} all-to-all(f32[1,2,8,2048]{3,1,0,2:T(2,128)S(1)} %bitcast.281), channel_id=1, replica_groups=mesh['gx'=8,'gy'=4] {'gx'}, dimensions={2} | all-to-all | bytes 262144 | tf_op jit(solution)/shard_map/all_to_all | solution.py:88
  268.5 9.7 %all_to_all.123 = f32[8,2,1,2048]{3,1,2,0:T(2,128)S(1)} all-to-all(f32[8,2,1,2048]{3,1,2,0:T(2,128)S(1)} %copy.37), channel_id=1, replica_groups=mesh['gx'=8,'gy'=4] {'gx'}, dimensions={0} | all-to-all | bytes 262144 | tf_op jit(solution)/shard_map/all_to_all | solution.py:93
  278.3 1.9 multiply_add_fusion.3
  280.6 2.4 fusion.50
  283.0 2.1 collective-permute-start.4
  285.1 3.6 %copy.47 = f32[4,8,64,256]{3,2,1,0:T(8,128)} copy(f32[4,8,64,256]{3,1,2,0:T(8,128)} %bitcast.264) | data formatting | bytes 4194304
  288.8 1.3 collective-permute-start.5
  290.1 6.8 %multiply_add_fusion = (f32[32,64,256]{2,1,0:T(8,128)}, f32[32,64,256]{2,1,0:T(8,128)S(1)}) fusion(f32[32,64,256]{2,1,0:T(8,128)} %param.21, f32[32,64,256]{2,1,0:T(8,128)} %param.20, f32[4,8,64,256]{3,2,1,0:T(8,128)} %copy.47, f32[32,64,256]{2,1,0:T(8,128)} %param.25, f32[4,8,64,256]{3,2,1,0:T(8,128)S(1)} %copy.43, f32[32,64,256]{2,1,0:T(8,128)} %param.23, ...), kind=kLoop, calls=%fused_computation.64 | loop fusion | flops 13631488 | bytes 18874368 | tf_op jit(solution)/shard_map/add | solution.py:229
  296.8 0.7 fusion.48
  297.9 1.3 collective-permute-start.6
  299.2 1.7 collective-permute-start.7
  302.3 1.4 copy-done.9
  305.3 0.8 copy-done.6
  306.7 4.8 %fusion.13 = f32[32,64,256]{2,1,0:T(8,128)} fusion(f32[32,64,256]{2,1,0:T(8,128)S(1)} %copy-done.6, f32[31,64,256]{2,1,0:T(8,128)S(1)} %slice.440, f32[1,64,256]{2,1,0:T(8,128)S(1)} %collective-permute-done.4, f32[1,64,256]{2,1,0:T(8,128)S(1)} %collective-permute-done.5, f32[31,64,256]{2,1,0:T(8,128)S(1)} %slice.441, ...), kind=kLoop, calls=%fused_computation.35 | loop fusion | flops 18350080 | bytes 25152256 | tf_op jit(solution)/shard_map/add | solution.py:228
  (296 shorter events, 67.1 us)
Async XLA Ops:
  0.6 1.0 copy-start
  0.6 4.4 %copy-start.19 = (f32[64,64]{1,0:T(8,128)S(1)}, f32[64,64]{1,0:T(8,128)}, u32[]{:S(2)}) copy-start(f32[64,64]{1,0:T(8,128)} %param.29) | copy-start | bytes 49156
  5.1 7.2 %copy-start.22 = (f32[65]{0:T(128)S(1)}, f32[65]{0:T(128)}, u32[]{:S(2)}) copy-start(f32[65]{0:T(128)} %param.28) | copy-start | bytes 784
  5.1 9.7 %copy-start.25 = (u32[32]{0:T(128)S(1)}, u32[32]{0:T(128)}, u32[]{:S(2)}) copy-start(u32[32]{0:T(128)} %constant.143) | copy-start | bytes 388
  5.1 55.3 %copy-start.21 = (f32[33]{0:T(128)S(1)}, f32[33]{0:T(128)}, u32[]{:S(2)}) copy-start(f32[33]{0:T(128)} %param.26) | copy-start | bytes 400
  5.1 55.9 %copy-start.24 = (u32[32]{0:T(128)S(1)}, u32[32]{0:T(128)}, u32[]{:S(2)}) copy-start(u32[32]{0:T(128)} %constant.148) | copy-start | bytes 388
  5.1 57.2 %copy-start.20 = (f32[32,32]{1,0:T(8,128)S(1)}, f32[32,32]{1,0:T(8,128)}, u32[]{:S(2)}) copy-start(f32[32,32]{1,0:T(8,128)} %param.27) | copy-start | bytes 12292
  7.9 159.4 %all-to-all-start = ((f32[1,2,4,2048]{3,1,0,2:T(2,128)}), f32[1,2,4,2048]{3,1,0,2:T(2,128)S(1)}, u32[]{:S(2)}, u32[]{:S(2)}) async-start(f32[1,2,4,2048]{3,1,0,2:T(2,128)} %pad_maximum_fusion.2), calls=%async_computation | async-start | bytes 131072 | tf_op jit(solution)/shard_map/all_to_all | solution.py:103
  168.3 7.4 %all-to-all-start.1 = ((f32[4,2,1,2048]{3,1,2,0:T(2,128)}), f32[4,2,1,2048]{3,1,2,0:T(2,128)S(1)}, u32[]{:S(2)}, u32[]{:S(2)}) async-start(f32[4,2,1,2048]{3,1,2,0:T(2,128)} %copy.29), calls=%async_computation.1 | async-start | bytes 131072 | tf_op jit(solution)/shard_map/all_to_all | solution.py:108
  177.5 18.2 %copy-start.23 = (f32[257]{0:T(512)S(1)}, f32[257]{0:T(512)}, u32[]{:S(2)}) copy-start(f32[257]{0:T(512)} %param.30) | copy-start | bytes 3088
  180.3 10.7 %all-to-all-start.2 = ((f32[1,2,8,2048]{3,1,0,2:T(2,128)}), f32[1,2,8,2048]{3,1,0,2:T(2,128)S(1)}, u32[]{:S(2)}, u32[]{:S(2)}) async-start(f32[1,2,8,2048]{3,1,0,2:T(2,128)} %bitcast.33), calls=%async_computation.2 | async-start | bytes 262144 | tf_op jit(solution)/shard_map/all_to_all | solution.py:88
  192.1 10.7 %all-to-all-start.3 = ((f32[8,2,1,2048]{3,1,2,0:T(2,128)}), f32[8,2,1,2048]{3,1,2,0:T(2,128)S(1)}, u32[]{:S(2)}, u32[]{:S(2)}) async-start(f32[8,2,1,2048]{3,1,2,0:T(2,128)} %copy.31), calls=%async_computation.3 | async-start | bytes 262144 | tf_op jit(solution)/shard_map/all_to_all | solution.py:93
  203.3 2.7 copy-start.4
  206.0 6.4 %collective-permute-start = (f32[1,64,256]{2,1,0:T(8,128)S(1)}, f32[1,64,256]{2,1,0:T(8,128)S(1)}, u32[]{:S(2)}, u32[]{:S(2)}) collective-permute-start(f32[1,64,256]{2,1,0:T(8,128)S(1)} %slice.354), channel_id=1, source_target_pairs={{0,4},{4,8},{8,12},{12,16},{16,20},{20,24},{24,28},{1,5},{5,9},{9,... | collective-permute-start | bytes 196616 | tf_op jit(solution)/shard_map/ppermute | solution.py:19
  210.4 6.2 %collective-permute-start.1 = (f32[1,64,256]{2,1,0:T(8,128)S(1)}, f32[1,64,256]{2,1,0:T(8,128)S(1)}, u32[]{:S(2)}, u32[]{:S(2)}) collective-permute-start(f32[1,64,256]{2,1,0:T(8,128)S(1)} %slice.361), channel_id=1, source_target_pairs={{4,0},{8,4},{12,8},{16,12},{20,16},{24,20},{28,24},{5,1},{9,5},{13... | collective-permute-start | bytes 196616 | tf_op jit(solution)/shard_map/ppermute | solution.py:22
  216.6 6.4 %collective-permute-start.2 = (f32[34,1,256]{2,1,0:T(1,128)S(1)}, f32[34,1,256]{2,1,0:T(1,128)S(1)}, u32[]{:S(2)}, u32[]{:S(2)}) collective-permute-start(f32[34,1,256]{2,1,0:T(1,128)S(1)} %get-tuple-element.777), channel_id=1, source_target_pairs={{0,1},{1,2},{2,3},{4,5},{5,6},{6,7},{8,9},{9,10},{10,11},{12,13},{... | collective-permute-start | bytes 104456 | tf_op jit(solution)/shard_map/ppermute | solution.py:19
  217.9 1.9 copy-start.12
  217.9 5.1 %collective-permute-start.3 = (f32[34,1,256]{2,1,0:T(1,128)S(1)}, f32[34,1,256]{2,1,0:T(1,128)S(1)}, u32[]{:S(2)}, u32[]{:S(2)}) collective-permute-start(f32[34,1,256]{2,1,0:T(1,128)S(1)} %get-tuple-element.776), channel_id=1, source_target_pairs={{1,0},{2,1},{3,2},{5,4},{6,5},{7,6},{9,8},{10,9},{11,10},{13,12},{... | collective-permute-start | bytes 104456 | tf_op jit(solution)/shard_map/ppermute | solution.py:22
  220.5 1.6 copy-start.11
  222.1 1.6 copy-start.15
  222.1 2.2 copy-start.18
  222.7 2.4 copy-start.13
  222.7 3.0 copy-start.14
  229.4 1.9 copy-start.5
  233.4 1.3 copy-start.8
  255.4 1.3 copy-start.7
  280.3 2.7 copy-start.3
  283.0 14.6 %collective-permute-start.4 = (f32[1,64,256]{2,1,0:T(8,128)S(1)}, f32[1,64,256]{2,1,0:T(8,128)S(1)}, u32[]{:S(2)}, u32[]{:S(2)}) collective-permute-start(f32[1,64,256]{2,1,0:T(8,128)S(1)} %slice.383), channel_id=1, source_target_pairs={{0,4},{4,8},{8,12},{12,16},{16,20},{20,24},{24,28},{1,5},{5,9},{9,... | collective-permute-start | bytes 196616 | tf_op jit(solution)/shard_map/ppermute | solution.py:19
  288.8 9.1 %collective-permute-start.5 = (f32[1,64,256]{2,1,0:T(8,128)S(1)}, f32[1,64,256]{2,1,0:T(8,128)S(1)}, u32[]{:S(2)}, u32[]{:S(2)}) collective-permute-start(f32[1,64,256]{2,1,0:T(8,128)S(1)} %slice.389), channel_id=1, source_target_pairs={{4,0},{8,4},{12,8},{16,12},{20,16},{24,20},{28,24},{5,1},{9,5},{13... | collective-permute-start | bytes 196616 | tf_op jit(solution)/shard_map/ppermute | solution.py:22
  290.1 6.8 %copy-start.2 = (f32[4,8,64,256]{3,2,1,0:T(8,128)S(1)}, f32[4,8,64,256]{3,2,1,0:T(8,128)}, u32[]{:S(2)}) copy-start(f32[4,8,64,256]{3,2,1,0:T(8,128)} %copy.47) | copy-start | bytes 6291460
  297.9 6.7 %collective-permute-start.6 = (f32[34,1,256]{2,1,0:T(1,128)S(1)}, f32[34,1,256]{2,1,0:T(1,128)S(1)}, u32[]{:S(2)}, u32[]{:S(2)}) collective-permute-start(f32[34,1,256]{2,1,0:T(1,128)S(1)} %get-tuple-element.775), channel_id=1, source_target_pairs={{0,1},{1,2},{2,3},{4,5},{5,6},{6,7},{8,9},{9,10},{10,11},{12,13},{... | collective-permute-start | bytes 104456 | tf_op jit(solution)/shard_map/ppermute | solution.py:19
  299.2 2.2 copy-start.10
  299.2 5.4 %collective-permute-start.7 = (f32[34,1,256]{2,1,0:T(1,128)S(1)}, f32[34,1,256]{2,1,0:T(1,128)S(1)}, u32[]{:S(2)}, u32[]{:S(2)}) collective-permute-start(f32[34,1,256]{2,1,0:T(1,128)S(1)} %get-tuple-element.774), channel_id=1, source_target_pairs={{1,0},{2,1},{3,2},{5,4},{6,5},{7,6},{9,8},{10,9},{11,10},{13,12},{... | collective-permute-start | bytes 104456 | tf_op jit(solution)/shard_map/ppermute | solution.py:22
  302.1 1.6 copy-start.9
  303.7 1.6 copy-start.17
  304.3 1.8 copy-start.6
  304.4 2.4 copy-start.16
  306.7 4.8 %copy-start.1 = (f32[256,256]{1,0:T(8,128)S(1)}, f32[256,256]{1,0:T(8,128)}, u32[]{:S(2)}) copy-start(f32[256,256]{1,0:T(8,128)} %param.31) | copy-start | bytes 786436
where the time goes:
time: 316 us; the launch traced here: 312 us
  local copies, waits for them, and re-layouts  84.9 us (27%)
  blocking collectives  65.2 us (21%)
  loops' own time  58.8 us (19%)
  other arithmetic  36.5 us (12%)
  starting transfers between devices  26.9 us (9%)
  waiting for transfers between devices  22.2 us (7%)
  matrix products  14.1 us (4%)
    dynamic_slice x70, local copies, waits for them, and re-layouts, reduced_solve(): lax.scan(forward, start_state, inputs)  42.6 us
    another operation x2, loops' own time, reduced_solve(): lax.scan(forward, start_state, inputs)  33.1 us
    unnamed x2, blocking collectives  29.6 us
    another operation x2, loops' own time, reduced_solve(): lax.scan(backward, jnp.zeros_like(first_tip[0]), (tops, lows, corners, bo...  25.6 us
    unnamed x68, local copies, waits for them, and re-layouts  23.6 us
    all_to_all x1, blocking collectives, first_reduced(): lax.all_to_all(pieces, 'gx', split_axis=2, concat_axis=0, tiled=True)  11.1 us
    all_to_all x1, blocking collectives, first_reduced(): lax.all_to_all(answer, 'gx', split_axis=0, concat_axis=2, tiled=True)  9.74 us
    add x2, other arithmetic, per_device(): temp_adjoint = temp_adjoint - explicit_part * kick + rate_temp * source  8.54 us
  transfers between devices with their start and end apart: 12, of which 4 were waited for; matrix products, arithmetic and copies ran while one was open for 27% of the time, Pallas kernels for 0%

commit v1 on v0

v1 whole, which is shorter than its diff:
```python
import functools

import jax
import jax.numpy as jnp
from jax import lax
from jax.experimental import pallas as pl
from jax.experimental.pallas import tpu as pltpu
from jax.sharding import PartitionSpec as P

explicit_part = 2.0
heat_release = 100.0
cure_step = 0.5
arrhenius = 0.5
initial_rate = 0.1
highest = lax.Precision.HIGHEST
MESH = pl.DeviceIdType.MESH
MARGIN = 8


def dot(a, b):
    return jnp.dot(a, b, precision=highest, preferred_element_type=jnp.float32)


def reduced_coefficients(ends, coef, count):
    corner = None
    for k in range(count - 1):
        upper = ends[k, 3:4]
        if corner is not None:
            upper = upper + ends[k, 1:2] * ends[k, 2:3] * corner
        head = ends[k + 1, 0:1]
        bottom = 1.0 / (1.0 - upper * head)
        corner = upper * bottom
        right_next = ends[k + 1, 2:3]
        coef[k, 0:1] = bottom
        coef[k, 1:2] = corner
        coef[k, 2:3] = head * bottom
        coef[k, 3:4] = ends[k, 1:2]
        coef[k, 4:5] = bottom * right_next
        coef[k, 5:6] = corner * right_next


def reduced_solve(first, last, coef, count):
    tops, lows = [], []
    for k in range(count - 1):
        shifted = last(k)
        if k:
            shifted = shifted + coef[k, 3:4] * tops[-1]
        follow = first(k + 1)
        tops.append(coef[k, 0:1] * shifted + coef[k, 1:2] * follow)
        lows.append(coef[k, 2:3] * shifted + coef[k, 0:1] * follow)
    for k in range(count - 3, -1, -1):
        tops[k] = tops[k] + coef[k, 5:6] * lows[k + 1]
        lows[k] = lows[k] + coef[k, 4:5] * lows[k + 1]
    zero = jnp.zeros_like(first(0))
    return lows + [zero], [zero] + tops


def kernel(
    nx,
    ny,
    ts_hbm,
    cs_hbm,
    tm_hbm,
    cm_hbm,
    al_hbm,
    ac_hbm,
    cf,
    bxs,
    bx,
    c2,
    by,
    ct,
    iz,
    out_t,
    out_c,
    lu,
    lc,
    t_mid,
    c_mid,
    t_start,
    c_start,
    g,
    mu,
    u,
    cya,
    cyb,
    wy0,
    wy1,
    ly,
    ry,
    tm_coef,
    tc_coef,
    zr,
    exs,
    exr,
    eys,
    eyr,
    coefx,
    coefy,
    xas,
    xar,
    xbs,
    xbr,
    yas,
    yar,
    ybs,
    ybr,
    eas,
    ear,
    eay,
    ebs,
    ebr,
    ebx,
    load_sem,
    store_sem,
    gx_send,
    gx_recv,
    gy_send,
    gy_recv,
):
    lx, lyn, nz = lu.shape
    rx = lyn // nx
    ryn = lx // ny
    mex = lax.axis_index("gx")
    mey = lax.axis_index("gy")
    sides = {"gx": (nx, mex, gx_send, gx_recv), "gy": (ny, mey, gy_send, gy_recv)}

    barrier = pltpu.get_barrier_semaphore()
    for axis, (count, me, _, _) in sides.items():
        for k in range(1, count):
            pl.semaphore_signal(
                barrier,
                inc=1,
                device_id={axis: lax.rem(me + k, count)},
                device_id_type=MESH,
            )

    loads = [
        pltpu.make_async_copy(source, target, load_sem.at[n])
        for n, (source, target) in enumerate(
            (
                (al_hbm, lu),
                (tm_hbm, t_mid),
                (cm_hbm, c_mid),
                (ac_hbm, lc),
                (ts_hbm, t_start),
                (cs_hbm, c_start),
            )
        )
    ]
    for load in loads:
        load.start()

    started = []

    def exchange(axis, kind, source, target):
        count, me, send, recv = sides[axis]
        copies = []
        for k in range(1, count):
            peer = lax.rem(me + k, count)
            copy = pltpu.make_async_remote_copy(
                src_ref=source(peer),
                dst_ref=target,
                send_sem=send.at[kind, k],
                recv_sem=recv.at[kind, k],
                device_id={axis: peer},
                device_id_type=MESH,
            )
            copy.start()
            copies.append(copy)
        started.extend(copies)
        return copies

    def arrive(copies):
        for copy in copies:
            copy.wait_recv()

    def row(value):
        return jnp.broadcast_to(value, (1, nz))

    a0, a1 = cf[0], cf[lx]
    exs[...] = jnp.zeros_like(exs)
    eys[...] = jnp.zeros_like(eys)
    exs[0:1] = row(a0 * bxs[0, 0])
    exs[1:2] = row(a0 * bxs[0, lx - 1])
    exs[2:3] = row(a1 * bxs[lx - 1, 0])
    exs[3:4] = row(a1 * bxs[lx - 1, lx - 1])
    s0, s1 = c2[0], c2[lyn]
    eys[0:1] = row(by[0:1, 0:1]) * s0
    eys[1:2] = row(by[0:1, lyn - 1 : lyn]) * s0
    eys[2:3] = row(by[lyn - 1 : lyn, 0:1]) * s1
    eys[3:4] = row(by[lyn - 1 : lyn, lyn - 1 : lyn]) * s1
    pl.semaphore_wait(barrier, nx + ny - 2)
    ends_x = exchange("gx", 0, lambda peer: exs, exr.at[mex])
    ends_y = exchange("gy", 0, lambda peer: eys, eyr.at[mey])
    exr[mex] = exs[...]
    eyr[mey] = eys[...]

    def second_faces(j, carry):
        cya[pl.ds(j, 1)] = row(c2[j])
        cyb[pl.ds(j, 1)] = row(c2[j + 1])
        return carry

    lax.fori_loop(0, lyn, second_faces, 0)
    wy0[...] = jnp.broadcast_to(by[:, 0:1], (lyn, nz))
    wy1[...] = jnp.broadcast_to(by[:, lyn - 1 : lyn], (lyn, nz))
    ly[...] = wy0[...] * s0
    ry[...] = wy1[...] * s1
    eas[...] = jnp.zeros_like(eas)
    ebs[...] = jnp.zeros_like(ebs)
    zr[...] = jnp.zeros_like(zr)

    def eliminate(i, keep):
        partial = 1.0 + cf[i] * keep
        scale = 1.0 / (partial + cf[i + 1])
        tm_coef[i] = scale
        tc_coef[i] = cf[i + 1] * scale
        return partial * scale

    lax.fori_loop(0, lx, eliminate, jnp.ones((1, nz), jnp.float32))

    face_low = ct[:, 0:nz]
    face_high = ct[:, 1 : nz + 1]

    for step in range(2):
        temper, cure = ((t_mid, c_mid), (t_start, c_start))[step]
        if step == 0:
            loads[0].wait()

        def tips(i, carry):
            first, last = carry
            slab = lu[i]
            u[pl.ds(i, 1), 0:nz] = jnp.sum(slab * wy0[...], axis=0, keepdims=True)
            u[pl.ds(i, 1), nz : 2 * nz] = jnp.sum(slab * wy1[...], axis=0, keepdims=True)
            return first + bxs[i, 0] * slab, last + bxs[i, lx - 1] * slab

        empty = jnp.zeros((lyn, nz), jnp.float32)
        first, last = lax.fori_loop(0, lx, tips, (empty, empty))
        tip_x = dot(by[...], jnp.concatenate([first, last], axis=1))
        for d in range(nx):
            xas[step, d, 0] = tip_x[d * rx : (d + 1) * rx, 0:nz]
            xas[step, d, 1] = tip_x[d * rx : (d + 1) * rx, nz:]
        out_xa = exchange("gx", 1 + 3 * step, lambda peer: xas.at[step, peer], xar.at[step, mex])
        eas[step, 0:1] = tip_x[0:1, 0:nz]
        eas[step, 1:2] = tip_x[0:1, nz:]
        eas[step, 2:3] = tip_x[lyn - 1 : lyn, 0:nz]
        eas[step, 3:4] = tip_x[lyn - 1 : lyn, nz:]
        out_ea = exchange("gy", 3 + 3 * step, lambda peer: eas.at[step], ear.at[step, mey])
        tip_y = dot(bx[...], u[...])
        for d in range(ny):
            yas[step, d, 0] = tip_y[d * ryn : (d + 1) * ryn, 0:nz]
            yas[step, d, 1] = tip_y[d * ryn : (d + 1) * ryn, nz:]
        out_ya = exchange("gy", 1 + 3 * step, lambda peer: yas.at[step, peer], yar.at[step, mey])
        xar[step, mex] = xas[step, mex]
        yar[step, mey] = yas[step, mey]
        ear[step, mey] = eas[step]

        def forward(i, before):
            value = (dot(by[...], lu[i]) + cf[i] * before) * tm_coef[i]
            g[i] = value
            return value

        lax.fori_loop(0, lx, forward, empty)

        if step == 0:
            arrive(ends_x)
            arrive(ends_y)
            reduced_coefficients(exr, coefx, nx)
            reduced_coefficients(eyr, coefy, ny)
        arrive(out_xa)
        lows, tops = reduced_solve(
            lambda k: xar[step, k, 0], lambda k: xar[step, k, 1], coefx, nx
        )
        for d in range(nx):
            xbs[step, d, 0] = lows[d]
            xbs[step, d, 1] = tops[d]
        out_xb = exchange("gx", 2 + 3 * step, lambda peer: xbs.at[step, peer], xbr.at[step, mex])
        arrive(out_ea)
        lows, tops = reduced_solve(
            lambda k: ear[step, k, 0:2], lambda k: ear[step, k, 2:4], coefy, ny
        )
        for d in range(ny):
            eay[d, 0:2] = lows[d]
            eay[d, 2:4] = tops[d]
        edge = eay[mey]
        ebs[step, 0:1] = edge[0:1]
        ebs[step, 1:2] = edge[2:3]
        ebs[step, 2:3] = edge[1:2]
        ebs[step, 3:4] = edge[3:4]
        out_eb = exchange("gx", 3 + 3 * step, lambda peer: ebs.at[step], ebr.at[step, mex])
        arrive(out_ya)
        lows, tops = reduced_solve(
            lambda k: yar[step, k, 0], lambda k: yar[step, k, 1], coefy, ny
        )
        for d in range(ny):
            ybs[step, d, 0] = lows[d]
            ybs[step, d, 1] = tops[d]
        out_yb = exchange("gy", 2 + 3 * step, lambda peer: ybs.at[step, peer], ybr.at[step, mey])
        xbr[step, mex] = xbs[step, mex]
        ybr[step, mey] = ybs[step, mey]
        ebr[step, mex] = ebs[step]

        def backward(n, after):
            i = lx - 1 - n
            value = g[i] + tc_coef[i] * after
            g[i] = value
            return value

        lax.fori_loop(0, lx, backward, empty)

        wide = 8

        def through(n, carry):
            block = g[pl.ds(n * wide, wide)].reshape(wide * lyn, nz)
            done = dot(block, iz[...]).reshape(wide, lyn, nz)
            mu[pl.ds(1 + n * wide, wide), MARGIN : MARGIN + lyn] = done
            return carry

        lax.fori_loop(0, lx // wide, through, 0)

        if step == 0:
            for n in (1, 2, 3):
                loads[n].wait()
        else:
            loads[4].wait()
            loads[5].wait()

        def rates(i, carry):
            heating = jnp.exp(arrhenius * temper[i])
            value = cure[i]
            remain = 1.0 - value
            grown = initial_rate + value
            temper[i] = arrhenius * (heating * grown * remain * remain)
            cure[i] = heating * (remain * remain - 2.0 * grown * remain)
            return carry

        lax.fori_loop(0, lx, rates, 0)

        arrive(out_eb)
        lows, tops = reduced_solve(
            lambda k: ebr[step, k, 0:2], lambda k: ebr[step, k, 2:4], coefx, nx
        )
        for d in range(nx):
            ebx[d, 0:2] = lows[d]
            ebx[d, 2:4] = tops[d]
        arrive(out_xb)
        arrive(out_yb)
        for d in range(nx):
            zr[d * rx : (d + 1) * rx] = xbr[step, d, 0]
            zr[lyn + d * rx : lyn + (d + 1) * rx] = xbr[step, d, 1]
        base = 2 * lyn
        for d in range(ny):
            zr[base + d * ryn : base + (d + 1) * ryn] = ybr[step, d, 0]
            zr[base + lx + d * ryn : base + lx + (d + 1) * ryn] = ybr[step, d, 1]
        corner = base + 2 * lx
        zr[corner : corner + 4] = ebx[mex, 0:4]
        zr[...] = dot(zr[...], iz[...])
        next_next = zr[corner : corner + 1]
        next_prev = zr[corner + 1 : corner + 2]
        prev_next = zr[corner + 2 : corner + 3]
        prev_prev = zr[corner + 3 : corner + 4]
        inside = slice(MARGIN, MARGIN + lyn)
        mu[lx + 1, inside] = zr[0:lyn] + ly[...] * next_prev + ry[...] * next_next
        mu[0, inside] = zr[lyn : 2 * lyn] + ly[...] * prev_prev + ry[...] * prev_next

        def correct(i, carry):
            left = a0 * bxs[0, i]
            right = a1 * bxs[lx - 1, i]
            y_next = zr[pl.ds(base + i, 1)]
            y_prev = zr[pl.ds(base + lx + i, 1)]
            mu[i + 1, inside] = (
                mu[i + 1, inside]
                + left * mu[0, inside]
                + right * mu[lx + 1, inside]
                + ly[...] * y_prev
                + ry[...] * y_next
            )
            mu[i + 1, MARGIN - 1 : MARGIN] = y_prev + left * prev_prev + right * next_prev
            mu[i + 1, MARGIN + lyn : MARGIN + lyn + 1] = (
                y_next + left * prev_next + right * next_next
            )
            return carry

        lax.fori_loop(0, lx, correct, 0)

        chunk = 16
        lane = lax.broadcasted_iota(jnp.int32, (chunk, nz), 1)

        def update(i, carry):
            for y in range(0, lyn, chunk):
                here = slice(y, y + chunk)
                start = MARGIN + y
                value = mu[i + 1, start : start + chunk]
                below = jnp.where(lane == 0, 0.0, pltpu.roll(value, 1, 1))
                above = jnp.where(lane == nz - 1, 0.0, pltpu.roll(value, nz - 1, 1))
                kick = (
                    cf[i] * (value - mu[i, start : start + chunk])
                    + cf[i + 1] * (value - mu[i + 2, start : start + chunk])
                    + cya[here] * (value - mu[i + 1, start - 1 : start + chunk - 1])
                    + cyb[here] * (value - mu[i + 1, start + 1 : start + chunk + 1])
                    + face_low * (value - below)
                    + face_high * (value - above)
                )
                old = lc[i, here]
                source = heat_release * value + cure_step * old
                lu[i, here] = lu[i, here] - explicit_part * kick + temper[i, here] * source
                lc[i, here] = old + cure[i, here] * source
            return carry

        if step == 0:
            lax.fori_loop(0, lx, update, 0)
        else:
            parts = 4
            each = lx // parts
            stores = []
            for part in range(parts):
                lax.fori_loop(part * each, (part + 1) * each, update, 0)
                for n, (source, target) in enumerate(((lu, out_t), (lc, out_c))):
                    store = pltpu.make_async_copy(
                        source.at[pl.ds(part * each, each)],
                        target.at[pl.ds(part * each, each)],
                        store_sem.at[n, part],
                    )
                    store.start()
                    stores.append(store)
            for store in stores:
                store.wait()
    for copy in started:
        copy.wait_send()


def per_device(nx, ny, ts, cs, tm, cm, al, ac, cf, bx, c2, by, ct, iz):
    lx, lyn, nz = al.shape
    f32 = jnp.float32
    vm = pltpu.VMEM
    tile = (lx, lyn, nz)
    hbm = pl.BlockSpec(memory_space=pl.ANY)
    smem = pl.BlockSpec(memory_space=pltpu.SMEM)
    vmem = pl.BlockSpec(memory_space=pltpu.VMEM)
    rx, ryn = lyn // nx, lx // ny
    scratch = (
        [vm(tile, f32)] * 7
        + [vm((lx + 2, lyn + 2 * MARGIN, nz), f32), vm((lx, 2 * nz), f32)]
        + [vm((lyn, nz), f32)] * 6
        + [vm((lx, 1, nz), f32)] * 2
        + [vm((2 * lyn + 2 * lx + 8, nz), f32)]
        + [vm((8, nz), f32), vm((nx, 8, nz), f32), vm((8, nz), f32), vm((ny, 8, nz), f32)]
        + [vm((nx, 8, nz), f32), vm((ny, 8, nz), f32)]
        + [vm((2, nx, 2, rx, nz), f32)] * 4
        + [vm((2, ny, 2, ryn, nz), f32)] * 4
        + [vm((2, 8, nz), f32), vm((2, ny, 8, nz), f32), vm((ny, 8, nz), f32)]
        + [vm((2, 8, nz), f32), vm((2, nx, 8, nz), f32), vm((nx, 8, nz), f32)]
        + [pltpu.SemaphoreType.DMA((6,)), pltpu.SemaphoreType.DMA((2, 4))]
        + [pltpu.SemaphoreType.DMA((7, nx))] * 2
        + [pltpu.SemaphoreType.DMA((7, ny))] * 2
    )
    return pl.pallas_call(
        functools.partial(kernel, nx, ny),
        out_shape=(jax.ShapeDtypeStruct(tile, f32), jax.ShapeDtypeStruct(tile, f32)),
        in_specs=[hbm] * 6 + [smem, smem, vmem, smem, vmem, vmem, vmem],
        out_specs=(hbm, hbm),
        scratch_shapes=scratch,
        compiler_params=pltpu.CompilerParams(
            collective_id=0, has_side_effects=True, vmem_limit_bytes=50 * 1024 * 1024
        ),
    )(ts, cs, tm, cm, al, ac, cf, bx, bx, c2, by, ct.reshape(1, -1), iz)


def solution(mesh):
    tile = P("gx", "gy", None)
    placed = (tile,) * 6 + (P("gx"), P("gx", None), P("gy"), P("gy", None), P(), P())
    return jax.shard_map(
        functools.partial(per_device, mesh.shape["gx"], mesh.shape["gy"]),
        mesh=mesh,
        in_specs=placed,
        out_specs=(tile, tile),
        check_vma=False,
    )
```

time: 316 us -> 66 us (0.21); the launches traced: 312 us -> 65.6 us
  local copies, waits for them, and re-layouts: 84.9 us -> 8.08 us
  blocking collectives: 65.2 us -> 0 us
  loops' own time: 58.8 us -> 0 us
  Pallas kernels: 0 us -> 56.9 us
  other arithmetic: 36.5 us -> 0 us
  starting transfers between devices: 26.9 us -> 0 us
  waiting for transfers between devices: 22.2 us -> 0 us
  matrix products: 14.1 us -> 0 us
    another operation x4 -> x0, loops' own time: 58.8 us -> none  [the longest x2 33.1 us: reduced_solve(): lax.scan(forward, start_state, inputs)]
    pallas_call x0 -> x1, Pallas kernels: none -> 56.9 us  [per_device(): pl.pallas_call(functools.partial(kernel, nx, ny), out_shape=(jax.ShapeDty...]
    dynamic_slice x70 -> x0, local copies, waits for them, and re-layouts: 42.6 us -> none  [reduced_solve(): lax.scan(forward, start_state, inputs)]
    all_to_all x4 -> x0, blocking collectives: 35.7 us -> none  [the longest x1 11.1 us: first_reduced(): lax.all_to_all(pieces, 'gx', split_axis=2, concat_axis=0, tiled=True)]
    unnamed x2 -> x0, blocking collectives: 29.6 us -> none
    add x7 -> x0, other arithmetic: 20 us -> none  [the longest x2 8.54 us: per_device(): temp_adjoint = temp_adjoint - explicit_part * kick + rate_temp * source]
    all_to_all x4 -> x0, waiting for transfers between devices: 18.2 us -> none  [the longest x1 7.2 us: first_reduced(): lax.all_to_all(pieces, 'gx', split_axis=2, concat_axis=0, tiled=True)]
    unnamed x68 -> x14, local copies, waits for them, and re-layouts: 23.6 us -> 7.39 us
  transfers between devices with their start and end apart: 12 -> 0, of which waited for: 4 -> 0; matrix products, arithmetic and copies ran while one was open for 27% -> 0% of each run, Pallas kernels for 0% -> 0%
where the time goes in v1:
time: 66 us; the launch traced here: 65.6 us
  Pallas kernels  56.9 us (86%)
  local copies, waits for them, and re-layouts  8.08 us (12%)
    pallas_call x1, Pallas kernels, per_device(): pl.pallas_call(functools.partial(kernel, nx, ny), out_shape=(jax.ShapeDty...  56.9 us
    unnamed x14, local copies, waits for them, and re-layouts  7.39 us

profile of v1, /device:TPU:0, one launch (start us, length us, event | category | flops | bytes accessed | tf_op | source)
XLA Modules:
  0.0 65.6 jit_solution(6155226085871668896)
XLA Ops:
  0.6 0.7 %reshape.7.ct = f32[1,257]{1,0:T(1,128)S(1)} reshape(f32[257]{0:T(512)} %param.22) | data formatting | bytes 2056 | tf_op jit(solution)/shard_map/reshape | solution.py:466
  1.3 0.0 copy-start
  1.3 0.9 %copy-done = f32[256,256]{1,0:T(8,128)S(1)} copy-done((f32[256,256]{1,0:T(8,128)S(1)}, f32[256,256]{1,0:T(8,128)}, u32[]{:S(2)}) %copy-start) | copy-done | bytes 262168
  2.3 0.0 copy-start.1
  2.3 0.7 %copy-done.1 = f32[32,32]{1,0:T(8,128)S(1)} copy-done((f32[32,32]{1,0:T(8,128)S(1)}, f32[32,32]{1,0:T(8,128)}, u32[]{:S(2)}) %copy-start.1) | copy-done | bytes 4120
  3.0 0.0 copy-start.2
  3.0 0.8 %copy-done.2 = f32[64,64]{1,0:T(8,128)S(1)} copy-done((f32[64,64]{1,0:T(8,128)S(1)}, f32[64,64]{1,0:T(8,128)}, u32[]{:S(2)}) %copy-start.2) | copy-done | bytes 16408
  3.7 0.0 copy-start.3
  3.7 0.7 copy-done.3
  4.4 0.0 copy-start.4
  4.4 0.7 copy-done.4
  5.1 56.9 %shard_map.131 = (f32[32,64,256]{2,1,0:T(8,128)S(1)}, f32[32,64,256]{2,1,0:T(8,128)}) custom-call(f32[32,64,256]{2,1,0:T(8,128)} %ts_hbm.1, f32[32,64,256]{2,1,0:T(8,128)} %cs_hbm.1, f32[32,64,256]{2,1,0:T(8,128)} %tm_hbm.1, f32[32,64,256]{2,1,0:T(8,128)} %cm_hbm.1, f32[32,64,256]{2,1,0:T(8,128)} %al_hbm.1, f32[32,64,256]{2,1,0:T(8,128)} %ac_hbm.1, ...), custom_call_target="tpu_custom_call" | custom-call | tf_op jit(solution)/shard_map/pallas_call | solution.py:457
  62.0 0.0 copy-start.5
  62.0 1.3 %copy.16 = f32[32,64,256]{2,1,0:T(8,128)} copy(f32[32,64,256]{2,1,0:T(8,128)S(1)} %get-tuple-element.4) | data formatting | bytes 4194304
  63.3 1.0 %copy-done.5 = f32[32,64,256]{2,1,0:T(8,128)S(1)} copy-done((f32[32,64,256]{2,1,0:T(8,128)S(1)}, f32[32,64,256]{2,1,0:T(8,128)}, u32[]{:S(2)}) %copy-start.5) | copy-done | bytes 2097176
  64.3 1.3 %copy.17 = f32[32,64,256]{2,1,0:T(8,128)} copy(f32[32,64,256]{2,1,0:T(8,128)S(1)} %copy-done.5) | data formatting | bytes 4194304
Async XLA Ops:
  1.3 0.9 %copy-start = (f32[256,256]{1,0:T(8,128)S(1)}, f32[256,256]{1,0:T(8,128)}, u32[]{:S(2)}) copy-start(f32[256,256]{1,0:T(8,128)} %iz.1) | copy-start | bytes 786436
  2.3 0.7 %copy-start.1 = (f32[32,32]{1,0:T(8,128)S(1)}, f32[32,32]{1,0:T(8,128)}, u32[]{:S(2)}) copy-start(f32[32,32]{1,0:T(8,128)} %bx.1) | copy-start | bytes 12292
  3.0 0.8 %copy-start.2 = (f32[64,64]{1,0:T(8,128)S(1)}, f32[64,64]{1,0:T(8,128)}, u32[]{:S(2)}) copy-start(f32[64,64]{1,0:T(8,128)} %by.1) | copy-start | bytes 49156
  3.7 0.7 copy-start.3
  4.4 0.7 copy-start.4
  62.0 2.3 %copy-start.5 = (f32[32,64,256]{2,1,0:T(8,128)S(1)}, f32[32,64,256]{2,1,0:T(8,128)}, u32[]{:S(2)}) copy-start(f32[32,64,256]{2,1,0:T(8,128)} %get-tuple-element.5) | copy-start | bytes 6291460

commit v2 on v1

--- a/solution.py
+++ b/solution.py
@@ -64,6 +64,14 @@
     cm_hbm,
     al_hbm,
     ac_hbm,
+    cf_hbm,
+    bx_hbm,
+    c2_hbm,
+    by_hbm,
+    ct_hbm,
+    iz_hbm,
+    out_t,
+    out_c,
     cf,
     bxs,
     bx,
@@ -71,8 +79,6 @@
     by,
     ct,
     iz,
-    out_t,
-    out_c,
     lu,
     lc,
     t_mid,
@@ -82,6 +88,8 @@
     g,
     mu,
     u,
+    bycat,
+    izcat,
     cya,
     cyb,
     wy0,
@@ -139,7 +147,14 @@
         pltpu.make_async_copy(source, target, load_sem.at[n])
         for n, (source, target) in enumerate(
             (
+                (bx_hbm, bxs),
+                (by_hbm, by),
                 (al_hbm, lu),
+                (bx_hbm, bx),
+                (cf_hbm, cf),
+                (c2_hbm, c2),
+                (iz_hbm, iz),
+                (ct_hbm, ct),
                 (tm_hbm, t_mid),
                 (cm_hbm, c_mid),
                 (ac_hbm, lc),
@@ -178,75 +193,94 @@
     def row(value):
         return jnp.broadcast_to(value, (1, nz))
 
-    a0, a1 = cf[0], cf[lx]
-    exs[...] = jnp.zeros_like(exs)
-    eys[...] = jnp.zeros_like(eys)
-    exs[0:1] = row(a0 * bxs[0, 0])
-    exs[1:2] = row(a0 * bxs[0, lx - 1])
-    exs[2:3] = row(a1 * bxs[lx - 1, 0])
-    exs[3:4] = row(a1 * bxs[lx - 1, lx - 1])
-    s0, s1 = c2[0], c2[lyn]
-    eys[0:1] = row(by[0:1, 0:1]) * s0
-    eys[1:2] = row(by[0:1, lyn - 1 : lyn]) * s0
-    eys[2:3] = row(by[lyn - 1 : lyn, 0:1]) * s1
-    eys[3:4] = row(by[lyn - 1 : lyn, lyn - 1 : lyn]) * s1
-    pl.semaphore_wait(barrier, nx + ny - 2)
-    ends_x = exchange("gx", 0, lambda peer: exs, exr.at[mex])
-    ends_y = exchange("gy", 0, lambda peer: eys, eyr.at[mey])
-    exr[mex] = exs[...]
-    eyr[mey] = eys[...]
-
-    def second_faces(j, carry):
-        cya[pl.ds(j, 1)] = row(c2[j])
-        cyb[pl.ds(j, 1)] = row(c2[j + 1])
-        return carry
-
-    lax.fori_loop(0, lyn, second_faces, 0)
+    wide = 4
+    chunk = 16
+    bf16 = jnp.bfloat16
+
+    def prepare():
+        def second_faces(j, carry):
+            cya[pl.ds(j, 1)] = row(c2[j])
+            cyb[pl.ds(j, 1)] = row(c2[j + 1])
+            return carry
+
+        lax.fori_loop(0, lyn, second_faces, 0, unroll=8)
+        ly[...] = wy0[...] * s0
+        ry[...] = wy1[...] * s1
+
+        def eliminate(i, keep):
+            partial = 1.0 + cf[i] * keep
+            scale = 1.0 / (partial + cf[i + 1])
+            tm_coef[i] = scale
+            tc_coef[i] = cf[i + 1] * scale
+            return partial * scale
+
+        lax.fori_loop(0, lx, eliminate, jnp.ones((1, nz), jnp.float32), unroll=4)
+        matrix = by[...]
+        part0 = matrix.astype(bf16)
+        rest = matrix - part0.astype(jnp.float32)
+        part1 = rest.astype(bf16)
+        part2 = (rest - part1.astype(jnp.float32)).astype(bf16)
+        for n, part in enumerate((part0, part1, part2)):
+            bycat[n * lyn : (n + 1) * lyn] = jnp.concatenate([part, part], axis=1)
+        matrix = iz[...]
+        part0 = matrix.astype(bf16)
+        izcat[0] = part0
+        izcat[1] = (matrix - part0.astype(jnp.float32)).astype(bf16)
+
+    loads[0].wait()
+    loads[1].wait()
     wy0[...] = jnp.broadcast_to(by[:, 0:1], (lyn, nz))
     wy1[...] = jnp.broadcast_to(by[:, lyn - 1 : lyn], (lyn, nz))
-    ly[...] = wy0[...] * s0
-    ry[...] = wy1[...] * s1
     eas[...] = jnp.zeros_like(eas)
     ebs[...] = jnp.zeros_like(ebs)
     zr[...] = jnp.zeros_like(zr)
-
-    def eliminate(i, keep):
-        partial = 1.0 + cf[i] * keep
-        scale = 1.0 / (partial + cf[i + 1])
-        tm_coef[i] = scale
-        tc_coef[i] = cf[i + 1] * scale
-        return partial * scale
-
-    lax.fori_loop(0, lx, eliminate, jnp.ones((1, nz), jnp.float32))
-
-    face_low = ct[:, 0:nz]
-    face_high = ct[:, 1 : nz + 1]
+    exs[...] = jnp.zeros_like(exs)
+    eys[...] = jnp.zeros_like(eys)
+    empty = jnp.zeros((lyn, nz), jnp.float32)
+
+    def fold(value):
+        return jnp.sum(value.reshape(-1, 8, nz), axis=0)
+
+    loads[2].wait()
+
+    def tips(i, carry):
+        first, last = carry
+        slab = lu[i]
+        u[0, i] = fold(slab * wy0[...])
+        u[1, i] = fold(slab * wy1[...])
+        return first + bxs[i, 0] * slab, last + bxs[i, lx - 1] * slab
+
+    first, last = lax.fori_loop(0, lx, tips, (empty, empty))
 
     for step in range(2):
         temper, cure = ((t_mid, c_mid), (t_start, c_start))[step]
-        if step == 0:
-            loads[0].wait()
-
-        def tips(i, carry):
-            first, last = carry
-            slab = lu[i]
-            u[pl.ds(i, 1), 0:nz] = jnp.sum(slab * wy0[...], axis=0, keepdims=True)
-            u[pl.ds(i, 1), nz : 2 * nz] = jnp.sum(slab * wy1[...], axis=0, keepdims=True)
-            return first + bxs[i, 0] * slab, last + bxs[i, lx - 1] * slab
-
-        empty = jnp.zeros((lyn, nz), jnp.float32)
-        first, last = lax.fori_loop(0, lx, tips, (empty, empty))
         tip_x = dot(by[...], jnp.concatenate([first, last], axis=1))
         for d in range(nx):
             xas[step, d, 0] = tip_x[d * rx : (d + 1) * rx, 0:nz]
             xas[step, d, 1] = tip_x[d * rx : (d + 1) * rx, nz:]
+        if step == 0:
+            for n in (3, 4, 5):
+                loads[n].wait()
+            a0, a1 = cf[0], cf[lx]
+            exs[0:1] = row(a0 * bxs[0, 0])
+            exs[1:2] = row(a0 * bxs[0, lx - 1])
+            exs[2:3] = row(a1 * bxs[lx - 1, 0])
+            exs[3:4] = row(a1 * bxs[lx - 1, lx - 1])
+            s0, s1 = c2[0], c2[lyn]
+            eys[0:1] = row(by[0:1, 0:1]) * s0
+            eys[1:2] = row(by[0:1, lyn - 1 : lyn]) * s0
+            eys[2:3] = row(by[lyn - 1 : lyn, 0:1]) * s1
+            eys[3:4] = row(by[lyn - 1 : lyn, lyn - 1 : lyn]) * s1
+            pl.semaphore_wait(barrier, nx + ny - 2)
         out_xa = exchange("gx", 1 + 3 * step, lambda peer: xas.at[step, peer], xar.at[step, mex])
         eas[step, 0:1] = tip_x[0:1, 0:nz]
         eas[step, 1:2] = tip_x[0:1, nz:]
         eas[step, 2:3] = tip_x[lyn - 1 : lyn, 0:nz]
         eas[step, 3:4] = tip_x[lyn - 1 : lyn, nz:]
         out_ea = exchange("gy", 3 + 3 * step, lambda peer: eas.at[step], ear.at[step, mey])
-        tip_y = dot(bx[...], u[...])
+        tip_y = dot(
+            bx[...], jnp.concatenate([jnp.sum(u[0], axis=1), jnp.sum(u[1], axis=1)], axis=1)
+        )
         for d in range(ny):
             yas[step, d, 0] = tip_y[d * ryn : (d + 1) * ryn, 0:nz]
             yas[step, d, 1] = tip_y[d * ryn : (d + 1) * ryn, nz:]
@@ -255,12 +289,46 @@
         yar[step, mey] = yas[step, mey]
         ear[step, mey] = eas[step]
 
+        if step == 0:
+            ends_x = exchange("gx", 0, lambda peer: exs, exr.at[mex])
+            ends_y = exchange("gy", 0, lambda peer: eys, eyr.at[mey])
+            exr[mex] = exs[...]
+            eyr[mey] = eys[...]
+            loads[6].wait()
+            loads[7].wait()
+            prepare()
+            face_low = ct[:, 0:nz]
+            face_high = ct[:, 1 : nz + 1]
+
+        def through(n, carry):
+            block = lu[pl.ds(n * wide, wide)].reshape(wide * lyn, nz)
+            high = block.astype(bf16)
+            low = (block - high.astype(jnp.float32)).astype(bf16)
+            done = (
+                jnp.dot(high, izcat[1], preferred_element_type=jnp.float32)
+                + jnp.dot(low, izcat[0], preferred_element_type=jnp.float32)
+                + jnp.dot(high, izcat[0], preferred_element_type=jnp.float32)
+            )
+            g[pl.ds(n * wide, wide)] = done.reshape(wide, lyn, nz)
+            return carry
+
+        lax.fori_loop(0, lx // wide, through, 0, unroll=2)
+
         def forward(i, before):
-            value = (dot(by[...], lu[i]) + cf[i] * before) * tm_coef[i]
+            slab = g[i]
+            high = slab.astype(bf16)
+            low = (slab - high.astype(jnp.float32)).astype(bf16)
+            stacked = jnp.dot(
+                bycat[...],
+                jnp.concatenate([high, low], axis=0),
+                preferred_element_type=jnp.float32,
+            )
+            solved = (stacked[2 * lyn :] + stacked[lyn : 2 * lyn]) + stacked[0:lyn]
+            value = (solved + cf[i] * before) * tm_coef[i]
             g[i] = value
             return value
 
-        lax.fori_loop(0, lx, forward, empty)
+        lax.fori_loop(0, lx, forward, empty, unroll=4)
 
         if step == 0:
             arrive(ends_x)
@@ -300,30 +368,22 @@
         ybr[step, mey] = ybs[step, mey]
         ebr[step, mex] = ebs[step]
 
+        inside = slice(MARGIN, MARGIN + lyn)
+
         def backward(n, after):
             i = lx - 1 - n
             value = g[i] + tc_coef[i] * after
-            g[i] = value
+            mu[i + 1, inside] = value
             return value
 
-        lax.fori_loop(0, lx, backward, empty)
-
-        wide = 8
-
-        def through(n, carry):
-            block = g[pl.ds(n * wide, wide)].reshape(wide * lyn, nz)
-            done = dot(block, iz[...]).reshape(wide, lyn, nz)
-            mu[pl.ds(1 + n * wide, wide), MARGIN : MARGIN + lyn] = done
-            return carry
-
-        lax.fori_loop(0, lx // wide, through, 0)
+        lax.fori_loop(0, lx, backward, empty, unroll=4)
 
         if step == 0:
-            for n in (1, 2, 3):
+            for n in (8, 9, 10):
                 loads[n].wait()
         else:
-            loads[4].wait()
-            loads[5].wait()
+            loads[11].wait()
+            loads[12].wait()
 
         def rates(i, carry):
             heating = jnp.exp(arrhenius * temper[i])
@@ -334,7 +394,7 @@
             cure[i] = heating * (remain * remain - 2.0 * grown * remain)
             return carry
 
-        lax.fori_loop(0, lx, rates, 0)
+        lax.fori_loop(0, lx, rates, 0, unroll=2)
 
         arrive(out_eb)
         lows, tops = reduced_solve(
@@ -359,7 +419,6 @@
         next_prev = zr[corner + 1 : corner + 2]
         prev_next = zr[corner + 2 : corner + 3]
         prev_prev = zr[corner + 3 : corner + 4]
-        inside = slice(MARGIN, MARGIN + lyn)
         mu[lx + 1, inside] = zr[0:lyn] + ly[...] * next_prev + ry[...] * next_next
         mu[0, inside] = zr[lyn : 2 * lyn] + ly[...] * prev_prev + ry[...] * prev_next
 
@@ -381,21 +440,23 @@
             )
             return carry
 
-        lax.fori_loop(0, lx, correct, 0)
-
-        chunk = 16
+        lax.fori_loop(0, lx, correct, 0, unroll=2)
+
         lane = lax.broadcasted_iota(jnp.int32, (chunk, nz), 1)
-
-        def update(i, carry):
-            for y in range(0, lyn, chunk):
-                here = slice(y, y + chunk)
-                start = MARGIN + y
-                value = mu[i + 1, start : start + chunk]
+        stores = []
+        firsts, lasts = [], []
+        for part, y in enumerate(range(0, lyn, chunk)):
+            here = slice(y, y + chunk)
+            start = MARGIN + y
+
+            def update(i, carry):
+                lower, value, first, last = carry
+                upper = mu[i + 2, start : start + chunk]
                 below = jnp.where(lane == 0, 0.0, pltpu.roll(value, 1, 1))
                 above = jnp.where(lane == nz - 1, 0.0, pltpu.roll(value, nz - 1, 1))
                 kick = (
-                    cf[i] * (value - mu[i, start : start + chunk])
-                    + cf[i + 1] * (value - mu[i + 2, start : start + chunk])
+                    cf[i] * (value - lower)
+                    + cf[i + 1] * (value - upper)
                     + cya[here] * (value - mu[i + 1, start - 1 : start + chunk - 1])
                     + cyb[here] * (value - mu[i + 1, start + 1 : start + chunk + 1])
                     + face_low * (value - below)
@@ -403,28 +464,39 @@
                 )
                 old = lc[i, here]
                 source = heat_release * value + cure_step * old
-                lu[i, here] = lu[i, here] - explicit_part * kick + temper[i, here] * source
+                new = lu[i, here] - explicit_part * kick + temper[i, here] * source
+                lu[i, here] = new
                 lc[i, here] = old + cure[i, here] * source
-            return carry
-
-        if step == 0:
-            lax.fori_loop(0, lx, update, 0)
-        else:
-            parts = 4
-            each = lx // parts
-            stores = []
-            for part in range(parts):
-                lax.fori_loop(part * each, (part + 1) * each, update, 0)
+                if step == 0:
+                    first = first + bxs[i, 0] * new
+                    last = last + bxs[i, lx - 1] * new
+                    for n, weight in enumerate((wy0, wy1)):
+                        folded = fold(new * weight[here])
+                        u[n, i] = folded if part == 0 else u[n, i] + folded
+                return upper, value, first, last
+
+            def ordered(i, carry):
+                upper, value, first, last = update(i, carry)
+                return value, upper, first, last
+
+            none = jnp.zeros((chunk, nz), jnp.float32)
+            begin = (mu[0, start : start + chunk], mu[1, start : start + chunk], none, none)
+            _, _, first, last = lax.fori_loop(0, lx, ordered, begin, unroll=2)
+            firsts.append(first)
+            lasts.append(last)
+            if step == 1:
                 for n, (source, target) in enumerate(((lu, out_t), (lc, out_c))):
                     store = pltpu.make_async_copy(
-                        source.at[pl.ds(part * each, each)],
-                        target.at[pl.ds(part * each, each)],
+                        source.at[:, pl.ds(y, chunk)],
+                        target.at[:, pl.ds(y, chunk)],
                         store_sem.at[n, part],
                     )
                     store.start()
                     stores.append(store)
-            for store in stores:
-                store.wait()
+        first = jnp.concatenate(firsts, axis=0)
+        last = jnp.concatenate(lasts, axis=0)
+        for store in stores:
+            store.wait()
     for copy in started:
         copy.wait_send()
 
@@ -434,13 +506,15 @@
     f32 = jnp.float32
     vm = pltpu.VMEM
     tile = (lx, lyn, nz)
-    hbm = pl.BlockSpec(memory_space=pl.ANY)
-    smem = pl.BlockSpec(memory_space=pltpu.SMEM)
-    vmem = pl.BlockSpec(memory_space=pltpu.VMEM)
+    hbm = pl.BlockSpec(memory_space=pltpu.HBM)
+    sm = pltpu.SMEM
     rx, ryn = lyn // nx, lx // ny
     scratch = (
-        [vm(tile, f32)] * 7
-        + [vm((lx + 2, lyn + 2 * MARGIN, nz), f32), vm((lx, 2 * nz), f32)]
+        [sm(cf.shape, f32), sm(bx.shape, f32), vm(bx.shape, f32), sm(c2.shape, f32)]
+        + [vm(by.shape, f32), vm((1, nz + 1), f32), vm(iz.shape, f32)]
+        + [vm(tile, f32)] * 7
+        + [vm((lx + 2, lyn + 2 * MARGIN, nz), f32), vm((2, lx, 8, nz), f32)]
+        + [vm((3 * lyn, 2 * lyn), jnp.bfloat16), vm((2, nz, nz), jnp.bfloat16)]
         + [vm((lyn, nz), f32)] * 6
         + [vm((lx, 1, nz), f32)] * 2
         + [vm((2 * lyn + 2 * lx + 8, nz), f32)]
@@ -450,20 +524,20 @@
         + [vm((2, ny, 2, ryn, nz), f32)] * 4
         + [vm((2, 8, nz), f32), vm((2, ny, 8, nz), f32), vm((ny, 8, nz), f32)]
         + [vm((2, 8, nz), f32), vm((2, nx, 8, nz), f32), vm((nx, 8, nz), f32)]
-        + [pltpu.SemaphoreType.DMA((6,)), pltpu.SemaphoreType.DMA((2, 4))]
+        + [pltpu.SemaphoreType.DMA((13,)), pltpu.SemaphoreType.DMA((2, lyn // 16))]
         + [pltpu.SemaphoreType.DMA((7, nx))] * 2
         + [pltpu.SemaphoreType.DMA((7, ny))] * 2
     )
     return pl.pallas_call(
         functools.partial(kernel, nx, ny),
         out_shape=(jax.ShapeDtypeStruct(tile, f32), jax.ShapeDtypeStruct(tile, f32)),
-        in_specs=[hbm] * 6 + [smem, smem, vmem, smem, vmem, vmem, vmem],
+        in_specs=[hbm] * 12,
         out_specs=(hbm, hbm),
         scratch_shapes=scratch,
         compiler_params=pltpu.CompilerParams(
-            collective_id=0, has_side_effects=True, vmem_limit_bytes=50 * 1024 * 1024
+            collective_id=0, has_side_effects=True, vmem_limit_bytes=56 * 1024 * 1024
         ),
-    )(ts, cs, tm, cm, al, ac, cf, bx, bx, c2, by, ct.reshape(1, -1), iz)
+    )(ts, cs, tm, cm, al, ac, cf, bx, c2, by, ct.reshape(1, -1), iz)
 
 
 def solution(mesh):

time: 66 us -> 69.2 us (1.048)
  Pallas kernels: 56.9 us -> 62.4 us
  local copies, waits for them, and re-layouts: 8.08 us -> 5.85 us
    pallas_call x1, Pallas kernels: 56.9 us -> 62.4 us  [per_device(): pl.pallas_call(functools.partial(kernel, nx, ny), out_shape=(jax.ShapeDty...]
    unnamed x14 -> x4, local copies, waits for them, and re-layouts: 7.39 us -> 4.6 us
where the time goes in v2:
time: 69.2 us; the launch traced here: 68.9 us
  Pallas kernels  62.4 us (90%)
  local copies, waits for them, and re-layouts  5.85 us (8%)
    pallas_call x1, Pallas kernels, per_device(): pl.pallas_call(functools.partial(kernel, nx, ny), out_shape=(jax.ShapeDty...  62.4 us
    unnamed x4, local copies, waits for them, and re-layouts  4.6 us

profile of v2, /device:TPU:0, one launch (start us, length us, event | category | flops | bytes accessed | tf_op | source)
XLA Modules:
  0.0 68.9 jit_solution(1753726856972822131)
XLA Ops:
  0.6 1.2 %reshape.7.ct_hbm = f32[1,257]{1,0:T(1,128)} reshape(f32[257]{0:T(512)} %param.22) | data formatting | bytes 2056 | tf_op jit(solution)/shard_map/reshape | solution.py:540
  1.9 62.4 %shard_map.131 = (f32[32,64,256]{2,1,0:T(8,128)}, f32[32,64,256]{2,1,0:T(8,128)}) custom-call(f32[32,64,256]{2,1,0:T(8,128)} %ts_hbm.1, f32[32,64,256]{2,1,0:T(8,128)} %cs_hbm.1, f32[32,64,256]{2,1,0:T(8,128)} %tm_hbm.1, f32[32,64,256]{2,1,0:T(8,128)} %cm_hbm.1, f32[32,64,256]{2,1,0:T(8,128)} %al_hbm.1, f32[32,64,256]{2,1,0:T(8,128)} %ac_hbm.1, f32[33]{0:T(128)} %cf_hbm.1, ...), custom_call_target="tpu_custom_call" | custom-call | tf_op jit(solution)/shard_map/pallas_call | solution.py:531
  64.3 0.0 copy-start
  64.3 3.3 %copy.16 = f32[32,64,256]{2,1,0:T(8,128)} copy(f32[32,64,256]{2,1,0:T(8,128)} %get-tuple-element.4) | data formatting | bytes 4194304
  67.6 0.0 copy-done
  67.6 1.3 %copy.17 = f32[32,64,256]{2,1,0:T(8,128)} copy(f32[32,64,256]{2,1,0:T(8,128)S(1)} %copy-done) | data formatting | bytes 4194304
Async XLA Ops:
  64.3 3.3 %copy-start = (f32[32,64,256]{2,1,0:T(8,128)S(1)}, f32[32,64,256]{2,1,0:T(8,128)}, u32[]{:S(2)}) copy-start(f32[32,64,256]{2,1,0:T(8,128)} %get-tuple-element.5) | copy-start | bytes 6291460

commit v3 on v2

--- a/solution.py
+++ b/solution.py
@@ -85,7 +85,14 @@
     c_mid,
     t_start,
     c_start,
+    lu_second,
+    lc_second,
+    rate_t,
+    rate_c,
     g,
+    h,
+    x_next,
+    x_prev,
     mu,
     u,
     bycat,
@@ -194,7 +201,7 @@
         return jnp.broadcast_to(value, (1, nz))
 
     wide = 4
-    chunk = 16
+    chunk = 32
     bf16 = jnp.bfloat16
 
     def prepare():
@@ -246,14 +253,16 @@
     def tips(i, carry):
         first, last = carry
         slab = lu[i]
-        u[0, i] = fold(slab * wy0[...])
-        u[1, i] = fold(slab * wy1[...])
+        u[0, 0, i] = fold(slab * wy0[...])
+        u[1, 0, i] = fold(slab * wy1[...])
         return first + bxs[i, 0] * slab, last + bxs[i, lx - 1] * slab
 
-    first, last = lax.fori_loop(0, lx, tips, (empty, empty))
+    first, last = lax.fori_loop(0, lx, tips, (empty, empty), unroll=4)
 
     for step in range(2):
         temper, cure = ((t_mid, c_mid), (t_start, c_start))[step]
+        lu_now, lc_now = ((lu, lc), (lu_second, lc_second))[step]
+        lu_then, lc_then = ((lu_second, lc_second), (lu, lc))[step]
         tip_x = dot(by[...], jnp.concatenate([first, last], axis=1))
         for d in range(nx):
             xas[step, d, 0] = tip_x[d * rx : (d + 1) * rx, 0:nz]
@@ -278,9 +287,8 @@
         eas[step, 2:3] = tip_x[lyn - 1 : lyn, 0:nz]
         eas[step, 3:4] = tip_x[lyn - 1 : lyn, nz:]
         out_ea = exchange("gy", 3 + 3 * step, lambda peer: eas.at[step], ear.at[step, mey])
-        tip_y = dot(
-            bx[...], jnp.concatenate([jnp.sum(u[0], axis=1), jnp.sum(u[1], axis=1)], axis=1)
-        )
+        folded = [u[n, 0] if step == 0 else u[n, 0] + u[n, 1] for n in range(2)]
+        tip_y = dot(bx[...], jnp.concatenate([jnp.sum(f, axis=1) for f in folded], axis=1))
         for d in range(ny):
             yas[step, d, 0] = tip_y[d * ryn : (d + 1) * ryn, 0:nz]
             yas[step, d, 1] = tip_y[d * ryn : (d + 1) * ryn, nz:]
@@ -297,11 +305,11 @@
             loads[6].wait()
             loads[7].wait()
             prepare()
-            face_low = ct[:, 0:nz]
-            face_high = ct[:, 1 : nz + 1]
+            face_low = ct[0:nz].reshape(1, nz)
+            face_high = ct[1 : nz + 1].reshape(1, nz)
 
         def through(n, carry):
-            block = lu[pl.ds(n * wide, wide)].reshape(wide * lyn, nz)
+            block = lu_now[pl.ds(n * wide, wide)].reshape(wide * lyn, nz)
             high = block.astype(bf16)
             low = (block - high.astype(jnp.float32)).astype(bf16)
             done = (
@@ -314,21 +322,25 @@
 
         lax.fori_loop(0, lx // wide, through, 0, unroll=2)
 
-        def forward(i, before):
-            slab = g[i]
-            high = slab.astype(bf16)
-            low = (slab - high.astype(jnp.float32)).astype(bf16)
-            stacked = jnp.dot(
-                bycat[...],
-                jnp.concatenate([high, low], axis=0),
-                preferred_element_type=jnp.float32,
-            )
-            solved = (stacked[2 * lyn :] + stacked[lyn : 2 * lyn]) + stacked[0:lyn]
-            value = (solved + cf[i] * before) * tm_coef[i]
-            g[i] = value
-            return value
-
-        lax.fori_loop(0, lx, forward, empty, unroll=4)
+        def forward(n, before):
+            solved = []
+            for k in range(wide):
+                slab = g[n * wide + k]
+                high = slab.astype(bf16)
+                low = (slab - high.astype(jnp.float32)).astype(bf16)
+                stacked = jnp.dot(
+                    bycat[...],
+                    jnp.concatenate([high, low], axis=0),
+                    preferred_element_type=jnp.float32,
+                )
+                solved.append((stacked[2 * lyn :] + stacked[lyn : 2 * lyn]) + stacked[0:lyn])
+            for k in range(wide):
+                i = n * wide + k
+                before = (solved[k] + cf[i] * before) * tm_coef[i]
+                h[i] = before
+            return before
+
+        lax.fori_loop(0, lx // wide, forward, empty)
 
         if step == 0:
             arrive(ends_x)
@@ -372,8 +384,8 @@
 
         def backward(n, after):
             i = lx - 1 - n
-            value = g[i] + tc_coef[i] * after
-            mu[i + 1, inside] = value
+            value = h[i] + tc_coef[i] * after
+            g[i] = value
             return value
 
         lax.fori_loop(0, lx, backward, empty, unroll=4)
@@ -390,8 +402,8 @@
             value = cure[i]
             remain = 1.0 - value
             grown = initial_rate + value
-            temper[i] = arrhenius * (heating * grown * remain * remain)
-            cure[i] = heating * (remain * remain - 2.0 * grown * remain)
+            rate_t[i] = arrhenius * (heating * grown * remain * remain)
+            rate_c[i] = heating * (remain * remain - 2.0 * grown * remain)
             return carry
 
         lax.fori_loop(0, lx, rates, 0, unroll=2)
@@ -419,8 +431,12 @@
         next_prev = zr[corner + 1 : corner + 2]
         prev_next = zr[corner + 2 : corner + 3]
         prev_prev = zr[corner + 3 : corner + 4]
-        mu[lx + 1, inside] = zr[0:lyn] + ly[...] * next_prev + ry[...] * next_next
-        mu[0, inside] = zr[lyn : 2 * lyn] + ly[...] * prev_prev + ry[...] * prev_next
+        value = zr[0:lyn] + ly[...] * next_prev + ry[...] * next_next
+        x_next[...] = value
+        mu[lx + 1, inside] = value
+        value = zr[lyn : 2 * lyn] + ly[...] * prev_prev + ry[...] * prev_next
+        x_prev[...] = value
+        mu[0, inside] = value
 
         def correct(i, carry):
             left = a0 * bxs[0, i]
@@ -428,9 +444,9 @@
             y_next = zr[pl.ds(base + i, 1)]
             y_prev = zr[pl.ds(base + lx + i, 1)]
             mu[i + 1, inside] = (
-                mu[i + 1, inside]
-                + left * mu[0, inside]
-                + right * mu[lx + 1, inside]
+                g[i]
+                + left * x_prev[...]
+                + right * x_next[...]
                 + ly[...] * y_prev
                 + ry[...] * y_next
             )
@@ -440,7 +456,7 @@
             )
             return carry
 
-        lax.fori_loop(0, lx, correct, 0, unroll=2)
+        lax.fori_loop(0, lx, correct, 0, unroll=4)
 
         lane = lax.broadcasted_iota(jnp.int32, (chunk, nz), 1)
         stores = []
@@ -450,38 +466,32 @@
             start = MARGIN + y
 
             def update(i, carry):
-                lower, value, first, last = carry
-                upper = mu[i + 2, start : start + chunk]
+                first, last = carry
+                value = mu[i + 1, start : start + chunk]
                 below = jnp.where(lane == 0, 0.0, pltpu.roll(value, 1, 1))
                 above = jnp.where(lane == nz - 1, 0.0, pltpu.roll(value, nz - 1, 1))
                 kick = (
-                    cf[i] * (value - lower)
-                    + cf[i + 1] * (value - upper)
+                    cf[i] * (value - mu[i, start : start + chunk])
+                    + cf[i + 1] * (value - mu[i + 2, start : start + chunk])
                     + cya[here] * (value - mu[i + 1, start - 1 : start + chunk - 1])
                     + cyb[here] * (value - mu[i + 1, start + 1 : start + chunk + 1])
                     + face_low * (value - below)
                     + face_high * (value - above)
                 )
-                old = lc[i, here]
+                old = lc_now[i, here]
                 source = heat_release * value + cure_step * old
-                new = lu[i, here] - explicit_part * kick + temper[i, here] * source
-                lu[i, here] = new
-                lc[i, here] = old + cure[i, here] * source
+                new = lu_now[i, here] - explicit_part * kick + rate_t[i, here] * source
+                lu_then[i, here] = new
+                lc_then[i, here] = old + rate_c[i, here] * source
                 if step == 0:
                     first = first + bxs[i, 0] * new
                     last = last + bxs[i, lx - 1] * new
-                    for n, weight in enumerate((wy0, wy1)):
-                        folded = fold(new * weight[here])
-                        u[n, i] = folded if part == 0 else u[n, i] + folded
-                return upper, value, first, last
-
-            def ordered(i, carry):
-                upper, value, first, last = update(i, carry)
-                return value, upper, first, last
+                    u[0, part, i] = fold(new * wy0[here])
+                    u[1, part, i] = fold(new * wy1[here])
+                return first, last
 
             none = jnp.zeros((chunk, nz), jnp.float32)
-            begin = (mu[0, start : start + chunk], mu[1, start : start + chunk], none, none)
-            _, _, first, last = lax.fori_loop(0, lx, ordered, begin, unroll=2)
+            first, last = lax.fori_loop(0, lx, update, (none, none), unroll=4)
             firsts.append(first)
             lasts.append(last)
             if step == 1:
@@ -501,19 +511,36 @@
         copy.wait_send()
 
 
+def hand_out(first, second, out_first, out_second, sem):
+    half = first.shape[0] // 2
+    copies = [
+        pltpu.make_async_copy(
+            source.at[pl.ds(part * half, half)], target.at[pl.ds(part * half, half)], sem.at[n, part]
+        )
+        for n, (source, target) in enumerate(((first, out_first), (second, out_second)))
+        for part in range(2)
+    ]
+    for copy in copies:
+        copy.start()
+    for copy in copies:
+        copy.wait()
+
+
 def per_device(nx, ny, ts, cs, tm, cm, al, ac, cf, bx, c2, by, ct, iz):
     lx, lyn, nz = al.shape
     f32 = jnp.float32
     vm = pltpu.VMEM
     tile = (lx, lyn, nz)
+    anywhere = pl.BlockSpec(memory_space=pl.ANY)
     hbm = pl.BlockSpec(memory_space=pltpu.HBM)
     sm = pltpu.SMEM
     rx, ryn = lyn // nx, lx // ny
     scratch = (
         [sm(cf.shape, f32), sm(bx.shape, f32), vm(bx.shape, f32), sm(c2.shape, f32)]
-        + [vm(by.shape, f32), vm((1, nz + 1), f32), vm(iz.shape, f32)]
-        + [vm(tile, f32)] * 7
-        + [vm((lx + 2, lyn + 2 * MARGIN, nz), f32), vm((2, lx, 8, nz), f32)]
+        + [vm(by.shape, f32), vm((nz + 1,), f32), vm(iz.shape, f32)]
+        + [vm(tile, f32)] * 12
+        + [vm((lyn, nz), f32)] * 2
+        + [vm((lx + 2, lyn + 2 * MARGIN, nz), f32), vm((2, 2, lx, 8, nz), f32)]
         + [vm((3 * lyn, 2 * lyn), jnp.bfloat16), vm((2, nz, nz), jnp.bfloat16)]
         + [vm((lyn, nz), f32)] * 6
         + [vm((lx, 1, nz), f32)] * 2
@@ -524,20 +551,28 @@
         + [vm((2, ny, 2, ryn, nz), f32)] * 4
         + [vm((2, 8, nz), f32), vm((2, ny, 8, nz), f32), vm((ny, 8, nz), f32)]
         + [vm((2, 8, nz), f32), vm((2, nx, 8, nz), f32), vm((nx, 8, nz), f32)]
-        + [pltpu.SemaphoreType.DMA((13,)), pltpu.SemaphoreType.DMA((2, lyn // 16))]
+        + [pltpu.SemaphoreType.DMA((13,)), pltpu.SemaphoreType.DMA((2, lyn // 32))]
         + [pltpu.SemaphoreType.DMA((7, nx))] * 2
         + [pltpu.SemaphoreType.DMA((7, ny))] * 2
     )
-    return pl.pallas_call(
+    results = pl.pallas_call(
         functools.partial(kernel, nx, ny),
         out_shape=(jax.ShapeDtypeStruct(tile, f32), jax.ShapeDtypeStruct(tile, f32)),
         in_specs=[hbm] * 12,
-        out_specs=(hbm, hbm),
+        out_specs=(anywhere, anywhere),
         scratch_shapes=scratch,
         compiler_params=pltpu.CompilerParams(
-            collective_id=0, has_side_effects=True, vmem_limit_bytes=56 * 1024 * 1024
+            collective_id=0, has_side_effects=True, vmem_limit_bytes=60 * 1024 * 1024
         ),
-    )(ts, cs, tm, cm, al, ac, cf, bx, c2, by, ct.reshape(1, -1), iz)
+    )(ts, cs, tm, cm, al, ac, cf, bx, c2, by, ct, iz)
+    return pl.pallas_call(
+        hand_out,
+        out_shape=(jax.ShapeDtypeStruct(tile, f32), jax.ShapeDtypeStruct(tile, f32)),
+        in_specs=[anywhere] * 2,
+        out_specs=(hbm, hbm),
+        scratch_shapes=[pltpu.SemaphoreType.DMA((2, 2))],
+        compiler_params=pltpu.CompilerParams(vmem_limit_bytes=1024 * 1024),
+    )(*results)
 
 
 def solution(mesh):

time: 69.2 us -> 49.3 us (0.71)
  Pallas kernels: 62.4 us -> 45.3 us
  local copies, waits for them, and re-layouts: 5.85 us -> 3.17 us
    pallas_call x1, Pallas kernels: 62.4 us -> 43.2 us  [per_device(): pl.pallas_call(functools.partial(kernel, nx, ny), out_shape=(jax.ShapeDty...]
    pallas_call x0 -> x1, Pallas kernels: none -> 2.04 us  [per_device(): pl.pallas_call(hand_out, out_shape=(jax.ShapeDtypeStruct(tile, f32), jax....]
    unnamed x4, local copies, waits for them, and re-layouts: 4.6 us -> 3.17 us
    reshape x1 -> x0, local copies, waits for them, and re-layouts: 1.25 us -> none  [per_device(): ct.reshape(1, -1)]
where the time goes in v3:
time: 49.3 us; the launch traced here: 49.1 us
  Pallas kernels  45.3 us (92%)
  local copies, waits for them, and re-layouts  3.17 us (6%)
  between operations  0.65 us (1%)
    pallas_call x1, Pallas kernels, per_device(): pl.pallas_call(functools.partial(kernel, nx, ny), out_shape=(jax.ShapeDty...  43.2 us
    unnamed x4, local copies, waits for them, and re-layouts  3.17 us
    pallas_call x1, Pallas kernels, per_device(): pl.pallas_call(hand_out, out_shape=(jax.ShapeDtypeStruct(tile, f32), jax....  2.04 us

profile of v3, /device:TPU:0, one launch (start us, length us, event | category | flops | bytes accessed | tf_op | source)
XLA Modules:
  0.0 49.1 jit_solution(7328585448611047845)
XLA Ops:
  0.6 43.2 %shard_map.131 = (f32[32,64,256]{2,1,0:T(8,128)}, f32[32,64,256]{2,1,0:T(8,128)}) custom-call(f32[32,64,256]{2,1,0:T(8,128)} %ts_hbm.1, f32[32,64,256]{2,1,0:T(8,128)} %cs_hbm.1, f32[32,64,256]{2,1,0:T(8,128)} %tm_hbm.1, f32[32,64,256]{2,1,0:T(8,128)} %cm_hbm.1, f32[32,64,256]{2,1,0:T(8,128)} %al_hbm.1, f32[32,64,256]{2,1,0:T(8,128)} %ac_hbm.1, f32[33]{0:T(128)} %cf_hbm.1, ...), custom_call_target="tpu_custom_call" | custom-call | tf_op jit(solution)/shard_map/pallas_call | solution.py:558
  43.9 0.0 copy-start
  43.9 1.6 %copy-done = f32[32,64,256]{2,1,0:T(8,128)S(1)} copy-done((f32[32,64,256]{2,1,0:T(8,128)S(1)}, f32[32,64,256]{2,1,0:T(8,128)}, u32[]{:S(2)}) %copy-start) | copy-done | bytes 2097176
  45.5 0.0 copy-start.1
  45.5 1.6 %copy-done.1 = f32[32,64,256]{2,1,0:T(8,128)S(1)} copy-done((f32[32,64,256]{2,1,0:T(8,128)S(1)}, f32[32,64,256]{2,1,0:T(8,128)}, u32[]{:S(2)}) %copy-start.1) | copy-done | bytes 2097176
  47.1 2.0 %shard_map.132 = (f32[32,64,256]{2,1,0:T(8,128)}, f32[32,64,256]{2,1,0:T(8,128)}) custom-call(f32[32,64,256]{2,1,0:T(8,128)S(1)} %copy-done, f32[32,64,256]{2,1,0:T(8,128)S(1)} %copy-done.1), custom_call_target="tpu_custom_call" | custom-call | tf_op jit(solution)/shard_map/pallas_call | solution.py:568
Async XLA Ops:
  43.9 1.6 %copy-start = (f32[32,64,256]{2,1,0:T(8,128)S(1)}, f32[32,64,256]{2,1,0:T(8,128)}, u32[]{:S(2)}) copy-start(f32[32,64,256]{2,1,0:T(8,128)} %get-tuple-element.4.first) | copy-start | bytes 6291460
  45.5 1.6 %copy-start.1 = (f32[32,64,256]{2,1,0:T(8,128)S(1)}, f32[32,64,256]{2,1,0:T(8,128)}, u32[]{:S(2)}) copy-start(f32[32,64,256]{2,1,0:T(8,128)} %get-tuple-element.5.second) | copy-start | bytes 6291460

commit v4 on v3

--- a/solution.py
+++ b/solution.py
@@ -12,13 +12,8 @@
 cure_step = 0.5
 arrhenius = 0.5
 initial_rate = 0.1
-highest = lax.Precision.HIGHEST
 MESH = pl.DeviceIdType.MESH
 MARGIN = 8
-
-
-def dot(a, b):
-    return jnp.dot(a, b, precision=highest, preferred_element_type=jnp.float32)
 
 
 def reduced_coefficients(ends, coef, count):
@@ -96,7 +91,10 @@
     mu,
     u,
     bycat,
+    bxcat,
     izcat,
+    diagonal,
+    thick,
     cya,
     cyb,
     wy0,
@@ -154,12 +152,12 @@
         pltpu.make_async_copy(source, target, load_sem.at[n])
         for n, (source, target) in enumerate(
             (
+                (cf_hbm, cf),
                 (bx_hbm, bxs),
                 (by_hbm, by),
+                (bx_hbm, bx),
+                (c2_hbm, c2),
                 (al_hbm, lu),
-                (bx_hbm, bx),
-                (cf_hbm, cf),
-                (c2_hbm, c2),
                 (iz_hbm, iz),
                 (ct_hbm, ct),
                 (tm_hbm, t_mid),
@@ -204,38 +202,54 @@
     chunk = 32
     bf16 = jnp.bfloat16
 
-    def prepare():
-        def second_faces(j, carry):
-            cya[pl.ds(j, 1)] = row(c2[j])
-            cyb[pl.ds(j, 1)] = row(c2[j + 1])
-            return carry
-
-        lax.fori_loop(0, lyn, second_faces, 0, unroll=8)
-        ly[...] = wy0[...] * s0
-        ry[...] = wy1[...] * s1
-
-        def eliminate(i, keep):
-            partial = 1.0 + cf[i] * keep
-            scale = 1.0 / (partial + cf[i + 1])
-            tm_coef[i] = scale
-            tc_coef[i] = cf[i + 1] * scale
-            return partial * scale
-
-        lax.fori_loop(0, lx, eliminate, jnp.ones((1, nz), jnp.float32), unroll=4)
-        matrix = by[...]
+    def stack(matrix, target):
+        size = matrix.shape[0]
         part0 = matrix.astype(bf16)
         rest = matrix - part0.astype(jnp.float32)
         part1 = rest.astype(bf16)
         part2 = (rest - part1.astype(jnp.float32)).astype(bf16)
         for n, part in enumerate((part0, part1, part2)):
-            bycat[n * lyn : (n + 1) * lyn] = jnp.concatenate([part, part], axis=1)
+            target[n * size : (n + 1) * size] = jnp.concatenate([part, part], axis=1)
+
+    def parted(value):
+        high = value.astype(bf16)
+        return high, (value - high.astype(jnp.float32)).astype(bf16)
+
+    def stacked_dot(parts, value):
+        size = value.shape[0]
+        done = jnp.dot(
+            parts[...],
+            jnp.concatenate(parted(value), axis=0),
+            preferred_element_type=jnp.float32,
+        )
+        return (done[2 * size :] + done[size : 2 * size]) + done[0:size]
+
+    def prepare():
+        face_low = explicit_part * ct[0:nz].reshape(1, nz)
+        face_high = explicit_part * ct[1 : nz + 1].reshape(1, nz)
+        lane = lax.broadcasted_iota(jnp.int32, (1, nz), 1)
+        thick[0:1] = jnp.where(lane == 0, 0.0, face_low)
+        thick[1:2] = jnp.where(lane == nz - 1, 0.0, face_high)
+        def second_faces(j, carry):
+            low, high = explicit_part * c2[j], explicit_part * c2[j + 1]
+            cya[pl.ds(j, 1)] = row(low)
+            cyb[pl.ds(j, 1)] = row(high)
+            diagonal[pl.ds(j, 1)] = face_low + face_high + (low + high)
+            return carry
+
+        lax.fori_loop(0, lyn, second_faces, 0, unroll=8)
+        ly[...] = wy0[...] * s0
+        ry[...] = wy1[...] * s1
+
         matrix = iz[...]
         part0 = matrix.astype(bf16)
         izcat[0] = part0
         izcat[1] = (matrix - part0.astype(jnp.float32)).astype(bf16)
 
-    loads[0].wait()
-    loads[1].wait()
+    for n in range(5):
+        loads[n].wait()
+    stack(by[...], bycat)
+    stack(bx[...], bxcat)
     wy0[...] = jnp.broadcast_to(by[:, 0:1], (lyn, nz))
     wy1[...] = jnp.broadcast_to(by[:, lyn - 1 : lyn], (lyn, nz))
     eas[...] = jnp.zeros_like(eas)
@@ -248,7 +262,15 @@
     def fold(value):
         return jnp.sum(value.reshape(-1, 8, nz), axis=0)
 
-    loads[2].wait()
+    def eliminate(i, keep):
+        partial = 1.0 + cf[i] * keep
+        scale = 1.0 / (partial + cf[i + 1])
+        tm_coef[i] = scale
+        tc_coef[i] = cf[i + 1] * scale
+        return partial * scale
+
+    lax.fori_loop(0, lx, eliminate, jnp.ones((1, nz), jnp.float32), unroll=4)
+    loads[5].wait()
 
     def tips(i, carry):
         first, last = carry
@@ -263,13 +285,11 @@
         temper, cure = ((t_mid, c_mid), (t_start, c_start))[step]
         lu_now, lc_now = ((lu, lc), (lu_second, lc_second))[step]
         lu_then, lc_then = ((lu_second, lc_second), (lu, lc))[step]
-        tip_x = dot(by[...], jnp.concatenate([first, last], axis=1))
+        tip_x = stacked_dot(bycat, jnp.concatenate([first, last], axis=1))
         for d in range(nx):
             xas[step, d, 0] = tip_x[d * rx : (d + 1) * rx, 0:nz]
             xas[step, d, 1] = tip_x[d * rx : (d + 1) * rx, nz:]
         if step == 0:
-            for n in (3, 4, 5):
-                loads[n].wait()
             a0, a1 = cf[0], cf[lx]
             exs[0:1] = row(a0 * bxs[0, 0])
             exs[1:2] = row(a0 * bxs[0, lx - 1])
@@ -288,7 +308,7 @@
         eas[step, 3:4] = tip_x[lyn - 1 : lyn, nz:]
         out_ea = exchange("gy", 3 + 3 * step, lambda peer: eas.at[step], ear.at[step, mey])
         folded = [u[n, 0] if step == 0 else u[n, 0] + u[n, 1] for n in range(2)]
-        tip_y = dot(bx[...], jnp.concatenate([jnp.sum(f, axis=1) for f in folded], axis=1))
+        tip_y = stacked_dot(bxcat, jnp.concatenate([jnp.sum(f, axis=1) for f in folded], axis=1))
         for d in range(ny):
             yas[step, d, 0] = tip_y[d * ryn : (d + 1) * ryn, 0:nz]
             yas[step, d, 1] = tip_y[d * ryn : (d + 1) * ryn, nz:]
@@ -305,13 +325,10 @@
             loads[6].wait()
             loads[7].wait()
             prepare()
-            face_low = ct[0:nz].reshape(1, nz)
-            face_high = ct[1 : nz + 1].reshape(1, nz)
 
         def through(n, carry):
             block = lu_now[pl.ds(n * wide, wide)].reshape(wide * lyn, nz)
-            high = block.astype(bf16)
-            low = (block - high.astype(jnp.float32)).astype(bf16)
+            high, low = parted(block)
             done = (
                 jnp.dot(high, izcat[1], preferred_element_type=jnp.float32)
                 + jnp.dot(low, izcat[0], preferred_element_type=jnp.float32)
@@ -323,24 +340,15 @@
         lax.fori_loop(0, lx // wide, through, 0, unroll=2)
 
         def forward(n, before):
-            solved = []
-            for k in range(wide):
-                slab = g[n * wide + k]
-                high = slab.astype(bf16)
-                low = (slab - high.astype(jnp.float32)).astype(bf16)
-                stacked = jnp.dot(
-                    bycat[...],
-                    jnp.concatenate([high, low], axis=0),
-                    preferred_element_type=jnp.float32,
-                )
-                solved.append((stacked[2 * lyn :] + stacked[lyn : 2 * lyn]) + stacked[0:lyn])
+            solved = [stacked_dot(bycat, g[n * wide + k]) for k in range(wide)]
             for k in range(wide):
                 i = n * wide + k
                 before = (solved[k] + cf[i] * before) * tm_coef[i]
                 h[i] = before
             return before
 
-        lax.fori_loop(0, lx // wide, forward, empty)
+        if step == 1:
+            lax.fori_loop(0, lx // wide, forward, empty)
 
         if step == 0:
             arrive(ends_x)
@@ -382,6 +390,9 @@
 
         inside = slice(MARGIN, MARGIN + lyn)
 
+        if step == 0:
+            lax.fori_loop(0, lx // wide, forward, empty)
+
         def backward(n, after):
             i = lx - 1 - n
             value = h[i] + tc_coef[i] * after
@@ -402,8 +413,8 @@
             value = cure[i]
             remain = 1.0 - value
             grown = initial_rate + value
-            rate_t[i] = arrhenius * (heating * grown * remain * remain)
-            rate_c[i] = heating * (remain * remain - 2.0 * grown * remain)
+            rate_t[i] = (heat_release * arrhenius) * (heating * grown * remain * remain)
+            rate_c[i] = (heat_release * heating) * (remain * remain - 2.0 * grown * remain)
             return carry
 
         lax.fori_loop(0, lx, rates, 0, unroll=2)
@@ -426,7 +437,19 @@
             zr[base + lx + d * ryn : base + lx + (d + 1) * ryn] = ybr[step, d, 1]
         corner = base + 2 * lx
         zr[corner : corner + 4] = ebx[mex, 0:4]
-        zr[...] = dot(zr[...], iz[...])
+        ends = zr[...]
+        high, low = parted(ends)
+        rest = ((ends - high.astype(jnp.float32)) - low.astype(jnp.float32)).astype(bf16)
+        count = ends.shape[0]
+        main = jnp.dot(
+            jnp.concatenate([high, low, rest], axis=0), izcat[0], preferred_element_type=jnp.float32
+        )
+        fine = jnp.dot(
+            jnp.concatenate([high, low], axis=0), izcat[1], preferred_element_type=jnp.float32
+        )
+        zr[...] = (
+            (main[2 * count :] + fine[count:]) + (main[count : 2 * count] + fine[0:count])
+        ) + main[0:count]
         next_next = zr[corner : corner + 1]
         next_prev = zr[corner + 1 : corner + 2]
         prev_next = zr[corner + 2 : corner + 3]
@@ -458,40 +481,48 @@
 
         lax.fori_loop(0, lx, correct, 0, unroll=4)
 
-        lane = lax.broadcasted_iota(jnp.int32, (chunk, nz), 1)
         stores = []
         firsts, lasts = [], []
+        group = 4
         for part, y in enumerate(range(0, lyn, chunk)):
             here = slice(y, y + chunk)
             start = MARGIN + y
 
-            def update(i, carry):
+            def update(n, carry):
                 first, last = carry
-                value = mu[i + 1, start : start + chunk]
-                below = jnp.where(lane == 0, 0.0, pltpu.roll(value, 1, 1))
-                above = jnp.where(lane == nz - 1, 0.0, pltpu.roll(value, nz - 1, 1))
-                kick = (
-                    cf[i] * (value - mu[i, start : start + chunk])
-                    + cf[i + 1] * (value - mu[i + 2, start : start + chunk])
-                    + cya[here] * (value - mu[i + 1, start - 1 : start + chunk - 1])
-                    + cyb[here] * (value - mu[i + 1, start + 1 : start + chunk + 1])
-                    + face_low * (value - below)
-                    + face_high * (value - above)
+                i = n * group
+                flux = (explicit_part * cf[i]) * (
+                    mu[i + 1, start : start + chunk] - mu[i, start : start + chunk]
                 )
-                old = lc_now[i, here]
-                source = heat_release * value + cure_step * old
-                new = lu_now[i, here] - explicit_part * kick + rate_t[i, here] * source
-                lu_then[i, here] = new
-                lc_then[i, here] = old + rate_c[i, here] * source
-                if step == 0:
-                    first = first + bxs[i, 0] * new
-                    last = last + bxs[i, lx - 1] * new
-                    u[0, part, i] = fold(new * wy0[here])
-                    u[1, part, i] = fold(new * wy1[here])
+                for k in range(group):
+                    i = n * group + k
+                    value = mu[i + 1, start : start + chunk]
+                    follow = (explicit_part * cf[i + 1]) * (
+                        mu[i + 2, start : start + chunk] - value
+                    )
+                    kick = (
+                        (flux - follow)
+                        + diagonal[here] * value
+                        - cya[here] * mu[i + 1, start - 1 : start + chunk - 1]
+                        - cyb[here] * mu[i + 1, start + 1 : start + chunk + 1]
+                        - thick[0:1] * pltpu.roll(value, 1, 1)
+                        - thick[1:2] * pltpu.roll(value, nz - 1, 1)
+                    )
+                    flux = follow
+                    old = lc_now[i, here]
+                    source = value + (cure_step / heat_release) * old
+                    new = lu_now[i, here] - kick + rate_t[i, here] * source
+                    lu_then[i, here] = new
+                    lc_then[i, here] = old + rate_c[i, here] * source
+                    if step == 0:
+                        first = first + bxs[i, 0] * new
+                        last = last + bxs[i, lx - 1] * new
+                        u[0, part, i] = fold(new * wy0[here])
+                        u[1, part, i] = fold(new * wy1[here])
                 return first, last
 
             none = jnp.zeros((chunk, nz), jnp.float32)
-            first, last = lax.fori_loop(0, lx, update, (none, none), unroll=4)
+            first, last = lax.fori_loop(0, lx // group, update, (none, none))
             firsts.append(first)
             lasts.append(last)
             if step == 1:
@@ -512,13 +543,13 @@
 
 
 def hand_out(first, second, out_first, out_second, sem):
-    half = first.shape[0] // 2
+    half = first.shape[0] // 4
     copies = [
         pltpu.make_async_copy(
             source.at[pl.ds(part * half, half)], target.at[pl.ds(part * half, half)], sem.at[n, part]
         )
         for n, (source, target) in enumerate(((first, out_first), (second, out_second)))
-        for part in range(2)
+        for part in range(4)
     ]
     for copy in copies:
         copy.start()
@@ -541,10 +572,11 @@
         + [vm(tile, f32)] * 12
         + [vm((lyn, nz), f32)] * 2
         + [vm((lx + 2, lyn + 2 * MARGIN, nz), f32), vm((2, 2, lx, 8, nz), f32)]
-        + [vm((3 * lyn, 2 * lyn), jnp.bfloat16), vm((2, nz, nz), jnp.bfloat16)]
+        + [vm((3 * lyn, 2 * lyn), jnp.bfloat16), vm((3 * lx, 2 * lx), jnp.bfloat16)]
+        + [vm((2, nz, nz), jnp.bfloat16), vm((lyn, nz), f32), vm((8, nz), f32)]
         + [vm((lyn, nz), f32)] * 6
         + [vm((lx, 1, nz), f32)] * 2
-        + [vm((2 * lyn + 2 * lx + 8, nz), f32)]
+        + [vm((2 * lyn + 2 * lx + 16, nz), f32)]
         + [vm((8, nz), f32), vm((nx, 8, nz), f32), vm((8, nz), f32), vm((ny, 8, nz), f32)]
         + [vm((nx, 8, nz), f32), vm((ny, 8, nz), f32)]
         + [vm((2, nx, 2, rx, nz), f32)] * 4
@@ -570,8 +602,8 @@
         out_shape=(jax.ShapeDtypeStruct(tile, f32), jax.ShapeDtypeStruct(tile, f32)),
         in_specs=[anywhere] * 2,
         out_specs=(hbm, hbm),
-        scratch_shapes=[pltpu.SemaphoreType.DMA((2, 2))],
-        compiler_params=pltpu.CompilerParams(vmem_limit_bytes=1024 * 1024),
+        scratch_shapes=[pltpu.SemaphoreType.DMA((2, 4))],
+        compiler_params=pltpu.CompilerParams(vmem_limit_bytes=60 * 1024 * 1024),
     )(*results)
 
 

time: 49.3 us -> 167 us (3.39)
  Pallas kernels: 45.3 us -> 166 us
  local copies, waits for them, and re-layouts: 3.17 us -> 0 us
    pallas_call x1, Pallas kernels: 2.04 us -> 128 us  [per_device(): pl.pallas_call(hand_out, out_shape=(jax.ShapeDtypeStruct(tile, f32), jax....]
    pallas_call x1, Pallas kernels: 43.2 us -> 38.2 us  [per_device(): pl.pallas_call(functools.partial(kernel, nx, ny), out_shape=(jax.ShapeDty...]
    unnamed x4 -> x0, local copies, waits for them, and re-layouts: 3.17 us -> none
where the time goes in v4:
time: 167 us
  Pallas kernels  166 us (99%)
    pallas_call x1, Pallas kernels, per_device(): pl.pallas_call(hand_out, out_shape=(jax.ShapeDtypeStruct(tile, f32), jax....  128 us
    pallas_call x1, Pallas kernels, per_device(): pl.pallas_call(functools.partial(kernel, nx, ny), out_shape=(jax.ShapeDty...  38.2 us

profile of v4, /device:TPU:0, one launch (start us, length us, event | category | flops | bytes accessed | tf_op | source)
XLA Modules:
  0.0 167.1 jit_solution(11913302759303699124)
XLA Ops:
  0.6 38.2 %shard_map.131 = (f32[32,64,256]{2,1,0:T(8,128)}, f32[32,64,256]{2,1,0:T(8,128)}) custom-call(f32[32,64,256]{2,1,0:T(8,128)} %ts_hbm.1, f32[32,64,256]{2,1,0:T(8,128)} %cs_hbm.1, f32[32,64,256]{2,1,0:T(8,128)} %tm_hbm.1, f32[32,64,256]{2,1,0:T(8,128)} %cm_hbm.1, f32[32,64,256]{2,1,0:T(8,128)} %al_hbm.1, f32[32,64,256]{2,1,0:T(8,128)} %ac_hbm.1, f32[33]{0:T(128)} %cf_hbm.1, ...), custom_call_target="tpu_custom_call" | custom-call | tf_op jit(solution)/shard_map/pallas_call | solution.py:590
  38.9 128.2 %shard_map.132 = (f32[32,64,256]{2,1,0:T(8,128)}, f32[32,64,256]{2,1,0:T(8,128)}) custom-call(f32[32,64,256]{2,1,0:T(8,128)} %get-tuple-element.4.first, f32[32,64,256]{2,1,0:T(8,128)} %get-tuple-element.5.second), custom_call_target="tpu_custom_call" | custom-call | tf_op jit(solution)/shard_map/pallas_call | solution.py:600

commit v5 on v4

--- a/solution.py
+++ b/solution.py
@@ -148,6 +148,7 @@
                 device_id_type=MESH,
             )
 
+    quarter = lx // 4
     loads = [
         pltpu.make_async_copy(source, target, load_sem.at[n])
         for n, (source, target) in enumerate(
@@ -157,7 +158,10 @@
                 (by_hbm, by),
                 (bx_hbm, bx),
                 (c2_hbm, c2),
-                (al_hbm, lu),
+                *(
+                    (al_hbm.at[pl.ds(k * quarter, quarter)], lu.at[pl.ds(k * quarter, quarter)])
+                    for k in range(4)
+                ),
                 (iz_hbm, iz),
                 (ct_hbm, ct),
                 (tm_hbm, t_mid),
@@ -199,6 +203,7 @@
         return jnp.broadcast_to(value, (1, nz))
 
     wide = 4
+    many = 8
     chunk = 32
     bf16 = jnp.bfloat16
 
@@ -270,8 +275,6 @@
         return partial * scale
 
     lax.fori_loop(0, lx, eliminate, jnp.ones((1, nz), jnp.float32), unroll=4)
-    loads[5].wait()
-
     def tips(i, carry):
         first, last = carry
         slab = lu[i]
@@ -279,7 +282,12 @@
         u[1, 0, i] = fold(slab * wy1[...])
         return first + bxs[i, 0] * slab, last + bxs[i, lx - 1] * slab
 
-    first, last = lax.fori_loop(0, lx, tips, (empty, empty), unroll=4)
+    first = last = empty
+    for k in range(4):
+        loads[5 + k].wait()
+        first, last = lax.fori_loop(
+            k * quarter, (k + 1) * quarter, tips, (first, last), unroll=4
+        )
 
     for step in range(2):
         temper, cure = ((t_mid, c_mid), (t_start, c_start))[step]
@@ -322,22 +330,22 @@
             ends_y = exchange("gy", 0, lambda peer: eys, eyr.at[mey])
             exr[mex] = exs[...]
             eyr[mey] = eys[...]
-            loads[6].wait()
-            loads[7].wait()
+            loads[9].wait()
+            loads[10].wait()
             prepare()
 
         def through(n, carry):
-            block = lu_now[pl.ds(n * wide, wide)].reshape(wide * lyn, nz)
+            block = lu_now[pl.ds(n * many, many)].reshape(many * lyn, nz)
             high, low = parted(block)
             done = (
                 jnp.dot(high, izcat[1], preferred_element_type=jnp.float32)
                 + jnp.dot(low, izcat[0], preferred_element_type=jnp.float32)
                 + jnp.dot(high, izcat[0], preferred_element_type=jnp.float32)
             )
-            g[pl.ds(n * wide, wide)] = done.reshape(wide, lyn, nz)
+            g[pl.ds(n * many, many)] = done.reshape(many, lyn, nz)
             return carry
 
-        lax.fori_loop(0, lx // wide, through, 0, unroll=2)
+        lax.fori_loop(0, lx // many, through, 0)
 
         def forward(n, before):
             solved = [stacked_dot(bycat, g[n * wide + k]) for k in range(wide)]
@@ -402,11 +410,11 @@
         lax.fori_loop(0, lx, backward, empty, unroll=4)
 
         if step == 0:
-            for n in (8, 9, 10):
+            for n in (11, 12, 13):
                 loads[n].wait()
         else:
-            loads[11].wait()
-            loads[12].wait()
+            loads[14].wait()
+            loads[15].wait()
 
         def rates(i, carry):
             heating = jnp.exp(arrhenius * temper[i])
@@ -522,18 +530,24 @@
                 return first, last
 
             none = jnp.zeros((chunk, nz), jnp.float32)
-            first, last = lax.fori_loop(0, lx // group, update, (none, none))
+            first = last = none
+            steps = lx // group // 2
+            for half in range(2):
+                first, last = lax.fori_loop(
+                    half * steps, (half + 1) * steps, update, (first, last)
+                )
+                if step == 1:
+                    rows = pl.ds(half * steps * group, steps * group)
+                    for n, (source, target) in enumerate(((lu, out_t), (lc, out_c))):
+                        store = pltpu.make_async_copy(
+                            source.at[rows, pl.ds(y, chunk)],
+                            target.at[rows, pl.ds(y, chunk)],
+                            store_sem.at[n, part, half],
+                        )
+                        store.start()
+                        stores.append(store)
             firsts.append(first)
             lasts.append(last)
-            if step == 1:
-                for n, (source, target) in enumerate(((lu, out_t), (lc, out_c))):
-                    store = pltpu.make_async_copy(
-                        source.at[:, pl.ds(y, chunk)],
-                        target.at[:, pl.ds(y, chunk)],
-                        store_sem.at[n, part],
-                    )
-                    store.start()
-                    stores.append(store)
         first = jnp.concatenate(firsts, axis=0)
         last = jnp.concatenate(lasts, axis=0)
         for store in stores:
@@ -542,18 +556,22 @@
         copy.wait_send()
 
 
-def hand_out(first, second, out_first, out_second, sem):
-    half = first.shape[0] // 4
-    copies = [
-        pltpu.make_async_copy(
-            source.at[pl.ds(part * half, half)], target.at[pl.ds(part * half, half)], sem.at[n, part]
-        )
-        for n, (source, target) in enumerate(((first, out_first), (second, out_second)))
-        for part in range(4)
-    ]
-    for copy in copies:
+def hand_out(first, second, out_first, out_second, held, sem):
+    chunks = held.shape[1]
+    size = first.shape[0] // chunks
+    arrivals, departures = [], []
+    for part in range(chunks):
+        rows = pl.ds(part * size, size)
+        for n, (source, target) in enumerate(((first, out_first), (second, out_second))):
+            slot = held.at[n, part]
+            arrivals.append(pltpu.make_async_copy(source.at[rows], slot, sem.at[0, n, part]))
+            departures.append(pltpu.make_async_copy(slot, target.at[rows], sem.at[1, n, part]))
+    for copy in arrivals:
         copy.start()
-    for copy in copies:
+    for arrival, departure in zip(arrivals, departures):
+        arrival.wait()
+        departure.start()
+    for copy in departures:
         copy.wait()
 
 
@@ -583,7 +601,7 @@
         + [vm((2, ny, 2, ryn, nz), f32)] * 4
         + [vm((2, 8, nz), f32), vm((2, ny, 8, nz), f32), vm((ny, 8, nz), f32)]
         + [vm((2, 8, nz), f32), vm((2, nx, 8, nz), f32), vm((nx, 8, nz), f32)]
-        + [pltpu.SemaphoreType.DMA((13,)), pltpu.SemaphoreType.DMA((2, lyn // 32))]
+        + [pltpu.SemaphoreType.DMA((16,)), pltpu.SemaphoreType.DMA((2, lyn // 32, 2))]
         + [pltpu.SemaphoreType.DMA((7, nx))] * 2
         + [pltpu.SemaphoreType.DMA((7, ny))] * 2
     )
@@ -602,7 +620,7 @@
         out_shape=(jax.ShapeDtypeStruct(tile, f32), jax.ShapeDtypeStruct(tile, f32)),
         in_specs=[anywhere] * 2,
         out_specs=(hbm, hbm),
-        scratch_shapes=[pltpu.SemaphoreType.DMA((2, 4))],
+        scratch_shapes=[vm((2, 8, lx // 8, lyn, nz), f32), pltpu.SemaphoreType.DMA((2, 2, 8))],
         compiler_params=pltpu.CompilerParams(vmem_limit_bytes=60 * 1024 * 1024),
     )(*results)
 

time: 167 us -> 42.7 us (0.26)
  Pallas kernels: 166 us -> 41.9 us
    pallas_call x1, Pallas kernels: 128 us -> 3.85 us  [per_device(): pl.pallas_call(hand_out, out_shape=(jax.ShapeDtypeStruct(tile, f32), jax....]
where the time goes in v5:
time: 42.7 us; the launch traced here: 42.5 us
  Pallas kernels  41.9 us (98%)
  between operations  0.64 us (1%)
    pallas_call x1, Pallas kernels, per_device(): pl.pallas_call(functools.partial(kernel, nx, ny), out_shape=(jax.ShapeDty...  38 us
    pallas_call x1, Pallas kernels, per_device(): pl.pallas_call(hand_out, out_shape=(jax.ShapeDtypeStruct(tile, f32), jax....  3.85 us

profile of v5, /device:TPU:0, one launch (start us, length us, event | category | flops | bytes accessed | tf_op | source)
XLA Modules:
  0.0 42.5 jit_solution(9371008708765629028)
XLA Ops:
  0.6 38.0 %shard_map.131 = (f32[32,64,256]{2,1,0:T(8,128)}, f32[32,64,256]{2,1,0:T(8,128)}) custom-call(f32[32,64,256]{2,1,0:T(8,128)} %ts_hbm.1, f32[32,64,256]{2,1,0:T(8,128)} %cs_hbm.1, f32[32,64,256]{2,1,0:T(8,128)} %tm_hbm.1, f32[32,64,256]{2,1,0:T(8,128)} %cm_hbm.1, f32[32,64,256]{2,1,0:T(8,128)} %al_hbm.1, f32[32,64,256]{2,1,0:T(8,128)} %ac_hbm.1, f32[33]{0:T(128)} %cf_hbm.1, ...), custom_call_target="tpu_custom_call" | custom-call | tf_op jit(solution)/shard_map/pallas_call | solution.py:608
  38.7 3.9 %shard_map.132 = (f32[32,64,256]{2,1,0:T(8,128)}, f32[32,64,256]{2,1,0:T(8,128)}) custom-call(f32[32,64,256]{2,1,0:T(8,128)} %get-tuple-element.4.first, f32[32,64,256]{2,1,0:T(8,128)} %get-tuple-element.5.second), custom_call_target="tpu_custom_call" | custom-call | tf_op jit(solution)/shard_map/pallas_call | solution.py:618

commit v6 on v5

--- a/solution.py
+++ b/solution.py
@@ -104,6 +104,7 @@
     tm_coef,
     tc_coef,
     zr,
+    zy,
     exs,
     exr,
     eys,
@@ -228,6 +229,20 @@
             preferred_element_type=jnp.float32,
         )
         return (done[2 * size :] + done[size : 2 * size]) + done[0:size]
+
+    def thick_dot(value):
+        count = value.shape[0]
+        high, low = parted(value)
+        rest = ((value - high.astype(jnp.float32)) - low.astype(jnp.float32)).astype(bf16)
+        main = jnp.dot(
+            jnp.concatenate([high, low, rest], axis=0), izcat[0], preferred_element_type=jnp.float32
+        )
+        fine = jnp.dot(
+            jnp.concatenate([high, low], axis=0), izcat[1], preferred_element_type=jnp.float32
+        )
+        return (
+            (main[2 * count :] + fine[count:]) + (main[count : 2 * count] + fine[0:count])
+        ) + main[0:count]
 
     def prepare():
         face_low = explicit_part * ct[0:nz].reshape(1, nz)
@@ -427,6 +442,18 @@
 
         lax.fori_loop(0, lx, rates, 0, unroll=2)
 
+        arrive(out_yb)
+        for d in range(ny):
+            zy[d * ryn : (d + 1) * ryn] = ybr[step, d, 0]
+            zy[lx + d * ryn : lx + (d + 1) * ryn] = ybr[step, d, 1]
+        zy[...] = thick_dot(zy[...])
+
+        def beside(i, carry):
+            h[i] = g[i] + ly[...] * zy[pl.ds(lx + i, 1)] + ry[...] * zy[pl.ds(i, 1)]
+            return carry
+
+        lax.fori_loop(0, lx, beside, 0, unroll=4)
+
         arrive(out_eb)
         lows, tops = reduced_solve(
             lambda k: ebr[step, k, 0:2], lambda k: ebr[step, k, 2:4], coefx, nx
@@ -435,29 +462,12 @@
             ebx[d, 0:2] = lows[d]
             ebx[d, 2:4] = tops[d]
         arrive(out_xb)
-        arrive(out_yb)
         for d in range(nx):
             zr[d * rx : (d + 1) * rx] = xbr[step, d, 0]
             zr[lyn + d * rx : lyn + (d + 1) * rx] = xbr[step, d, 1]
-        base = 2 * lyn
-        for d in range(ny):
-            zr[base + d * ryn : base + (d + 1) * ryn] = ybr[step, d, 0]
-            zr[base + lx + d * ryn : base + lx + (d + 1) * ryn] = ybr[step, d, 1]
-        corner = base + 2 * lx
+        corner = 2 * lyn
         zr[corner : corner + 4] = ebx[mex, 0:4]
-        ends = zr[...]
-        high, low = parted(ends)
-        rest = ((ends - high.astype(jnp.float32)) - low.astype(jnp.float32)).astype(bf16)
-        count = ends.shape[0]
-        main = jnp.dot(
-            jnp.concatenate([high, low, rest], axis=0), izcat[0], preferred_element_type=jnp.float32
-        )
-        fine = jnp.dot(
-            jnp.concatenate([high, low], axis=0), izcat[1], preferred_element_type=jnp.float32
-        )
-        zr[...] = (
-            (main[2 * count :] + fine[count:]) + (main[count : 2 * count] + fine[0:count])
-        ) + main[0:count]
+        zr[...] = thick_dot(zr[...])
         next_next = zr[corner : corner + 1]
         next_prev = zr[corner + 1 : corner + 2]
         prev_next = zr[corner + 2 : corner + 3]
@@ -472,15 +482,9 @@
         def correct(i, carry):
             left = a0 * bxs[0, i]
             right = a1 * bxs[lx - 1, i]
-            y_next = zr[pl.ds(base + i, 1)]
-            y_prev = zr[pl.ds(base + lx + i, 1)]
-            mu[i + 1, inside] = (
-                g[i]
-                + left * x_prev[...]
-                + right * x_next[...]
-                + ly[...] * y_prev
-                + ry[...] * y_next
-            )
+            y_next = zy[pl.ds(i, 1)]
+            y_prev = zy[pl.ds(lx + i, 1)]
+            mu[i + 1, inside] = h[i] + left * x_prev[...] + right * x_next[...]
             mu[i + 1, MARGIN - 1 : MARGIN] = y_prev + left * prev_prev + right * next_prev
             mu[i + 1, MARGIN + lyn : MARGIN + lyn + 1] = (
                 y_next + left * prev_next + right * next_next
@@ -594,7 +598,7 @@
         + [vm((2, nz, nz), jnp.bfloat16), vm((lyn, nz), f32), vm((8, nz), f32)]
         + [vm((lyn, nz), f32)] * 6
         + [vm((lx, 1, nz), f32)] * 2
-        + [vm((2 * lyn + 2 * lx + 16, nz), f32)]
+        + [vm((2 * lyn + 16, nz), f32), vm((2 * lx, nz), f32)]
         + [vm((8, nz), f32), vm((nx, 8, nz), f32), vm((8, nz), f32), vm((ny, 8, nz), f32)]
         + [vm((nx, 8, nz), f32), vm((ny, 8, nz), f32)]
         + [vm((2, nx, 2, rx, nz), f32)] * 4

time: 42.7 us -> 42 us (0.984)
  Pallas kernels: 41.9 us -> 41.2 us
    pallas_call x1, Pallas kernels: 38 us -> 37.4 us  [per_device(): pl.pallas_call(functools.partial(kernel, nx, ny), out_shape=(jax.ShapeDty...]
where the time goes in v6:
time: 42 us; the launch traced here: 41.9 us
  Pallas kernels  41.2 us (98%)
  between operations  0.64 us (2%)
    pallas_call x1, Pallas kernels, per_device(): pl.pallas_call(functools.partial(kernel, nx, ny), out_shape=(jax.ShapeDty...  37.4 us
    pallas_call x1, Pallas kernels, per_device(): pl.pallas_call(hand_out, out_shape=(jax.ShapeDtypeStruct(tile, f32), jax....  3.85 us

profile of v6, /device:TPU:0, one launch (start us, length us, event | category | flops | bytes accessed | tf_op | source)
XLA Modules:
  0.0 41.9 jit_solution(16416416458739437670)
XLA Ops:
  0.6 37.4 %shard_map.131 = (f32[32,64,256]{2,1,0:T(8,128)}, f32[32,64,256]{2,1,0:T(8,128)}) custom-call(f32[32,64,256]{2,1,0:T(8,128)} %ts_hbm.1, f32[32,64,256]{2,1,0:T(8,128)} %cs_hbm.1, f32[32,64,256]{2,1,0:T(8,128)} %tm_hbm.1, f32[32,64,256]{2,1,0:T(8,128)} %cm_hbm.1, f32[32,64,256]{2,1,0:T(8,128)} %al_hbm.1, f32[32,64,256]{2,1,0:T(8,128)} %ac_hbm.1, f32[33]{0:T(128)} %cf_hbm.1, ...), custom_call_target="tpu_custom_call" | custom-call | tf_op jit(solution)/shard_map/pallas_call | solution.py:612
  38.0 3.9 %shard_map.132 = (f32[32,64,256]{2,1,0:T(8,128)}, f32[32,64,256]{2,1,0:T(8,128)}) custom-call(f32[32,64,256]{2,1,0:T(8,128)} %get-tuple-element.4.first, f32[32,64,256]{2,1,0:T(8,128)} %get-tuple-element.5.second), custom_call_target="tpu_custom_call" | custom-call | tf_op jit(solution)/shard_map/pallas_call | solution.py:622
